TPU v7x, 512 devices: a whole 4x4x16 slice. The times are simulated.
512 devices in a mesh: pages: 128 (over x, z, core), queries: 4 (over y).
Axes of the slice: x: 4, y: 4, z: 16, core: 2. Of those that a mesh axis runs over, the one named last changes fastest.
Arguments:
- page_states: bfloat16 [256, 768, 1536], P('pages', None, 'queries'), may hold values from -6 to 6
- projection: bfloat16 [1536, 128], P('queries'), may hold values from -0.59765625 to 0.59765625
- query_tokens: bfloat16 [8192, 32, 128], P(('pages', 'queries')), may hold values from -0.29882812 to 0.29882812
- candidates: int32 [8192, 16], P(('pages', 'queries')), may hold values from 0 to 255, all different within a row; in each aligned block of 16 rows (0 to 15, 16 to 31, ...) at most 2 rows name the same one
- patch_index: int32 [8192, 16, 32], P(('pages', 'queries')), may hold values from 0 to 767
- teacher_logits: float32 [8192, 16], P(('pages', 'queries')), may hold values from -10 to 10
- page_slot: int32 [256], replicated, may hold values from 0 to 255, each once
Outputs:
- grad_queries: float32 [8192, 32, 128], P(('pages', 'queries'))
- grad_projection: float32 [1536, 128], P('queries')
Inputs may be any that keep to these rules, and one draw needn't show every extreme that they name: `candidates`: the 16 ids in one query's row differ. Among the 16 rows of one device no page id is listed more than 2 times, and in some device's rows one id is listed exactly 2 times. `page_slot`: each slot of 0 to 255 is taken by exactly one page id.
All inputs are finite; a program needn't handle non-finite values.
Results may differ from a plain program's by a relative error of at most 0.0052.
Values may be sent and summed in bfloat16 or wider, within the bound.
A program may use at most 64 MiB of HBM per device.

v0:
```python
import math

import jax
import jax.numpy as jnp
from jax import lax
from jax.sharding import PartitionSpec as P

SOFTMAX_HEAT = 0.5
EPSILON = 1e-06


def unit_rows(values):
    inverse = lax.rsqrt(jnp.sum(values * values, axis=-1, keepdims=True) + EPSILON)
    return (values * inverse, inverse)


def body(page_states, projection, query_tokens, candidates, patch_index, teacher_logits, page_slot):
    owner_count = lax.axis_size("pages")
    local_pages, patch_count, width_share = page_states.shape
    embed_width = projection.shape[1]
    query_rows, cand_count, tok_count = patch_index.shape
    page_amount_total = page_slot.shape[0]
    capacity = max(2, (query_rows * cand_count + page_amount_total - 1) // page_amount_total)
    flat_states = page_states.reshape(local_pages * patch_count, width_share)
    embedded = jnp.dot(
        lax.all_gather(flat_states, "queries", axis=1, tiled=True),
        lax.all_gather(projection.T, "queries", axis=1, tiled=True).T,
        preferred_element_type=jnp.float32,
    )
    unit_embed32, inv_embed = unit_rows(embedded)
    unit_embed = unit_embed32.astype(jnp.bfloat16)
    unit_query32, inv_query = unit_rows(query_tokens.astype(jnp.float32))
    unit_query = unit_query32.astype(jnp.bfloat16)
    pair_count = query_rows * cand_count
    flat_cand = candidates.reshape(pair_count)
    slot_ids = jnp.arange(page_amount_total, dtype=jnp.int32)
    page_row = jnp.sum(
        jnp.where(flat_cand[:, None] == slot_ids[None, :], page_slot[None, :], 0), axis=1
    )
    row_hits = (page_row[:, None] == slot_ids[None, :]).astype(jnp.int32)
    arrival = jnp.sum((jnp.cumsum(row_hits, axis=0) - row_hits) * row_hits, axis=1)
    bucket_span = owner_count * capacity
    slot_total = local_pages * bucket_span
    target_slot = (
        page_row % local_pages * bucket_span + page_row // local_pages * capacity + arrival
    )
    pair_query = jnp.broadcast_to(
        unit_query[:, None], (query_rows, cand_count, tok_count, embed_width)
    )
    pair_query = pair_query.reshape(pair_count, tok_count, embed_width)
    send_query = (
        jnp.zeros((slot_total, tok_count, embed_width), jnp.bfloat16)
        .at[target_slot]
        .set(pair_query)
    )
    send_query = send_query.reshape(local_pages, bucket_span, tok_count, embed_width)
    send_index = (
        jnp.zeros((slot_total, tok_count), jnp.int32)
        .at[target_slot]
        .set(patch_index.reshape(pair_count, tok_count))
    )
    send_index = send_index.reshape(local_pages, bucket_span, tok_count)
    recv_query, recv_index = (
        lax.all_to_all(send_query, "pages", split_axis=1, concat_axis=1, tiled=True),
        lax.all_to_all(send_index, "pages", split_axis=1, concat_axis=1, tiled=True),
    )
    page_base = (jnp.arange(local_pages, dtype=jnp.int32) * patch_count)[:, None, None]
    picked = jnp.take(unit_embed, recv_index + page_base, axis=0)
    returned = lax.all_to_all(picked, "pages", split_axis=1, concat_axis=1, tiled=True)
    pair_rows = returned.reshape(slot_total, tok_count, embed_width)[target_slot]
    pair_rows = pair_rows.reshape(query_rows, cand_count, tok_count, embed_width)
    score_matrix = jnp.einsum(
        "ntd,nctd->nc", unit_query, pair_rows, preferred_element_type=jnp.float32
    )
    student_logits = jnp.exp(score_matrix / SOFTMAX_HEAT)
    student_logits = student_logits / jnp.sum(student_logits, axis=1, keepdims=True)
    target_probs = jnp.exp(teacher_logits)
    target_probs = target_probs / jnp.sum(target_probs, axis=1, keepdims=True)
    weight_factor = ((student_logits - target_probs) / SOFTMAX_HEAT).astype(jnp.bfloat16)
    grad_unit = jnp.einsum(
        "nc,nctd->ntd", weight_factor, pair_rows, preferred_element_type=jnp.float32
    )
    grad_queries = (
        grad_unit - unit_query32 * jnp.sum(unit_query32 * grad_unit, axis=-1, keepdims=True)
    ) * inv_query
    send_weight = (
        jnp.zeros((slot_total,), jnp.bfloat16)
        .at[target_slot]
        .set(weight_factor.reshape(pair_count))
    )
    recv_weight = lax.all_to_all(
        send_weight.reshape(local_pages, bucket_span),
        "pages",
        split_axis=1,
        concat_axis=1,
        tiled=True,
    )
    row_total = bucket_span * tok_count
    block_rows = math.gcd(row_total, 1024)
    tok_query = recv_query.reshape(local_pages, row_total, embed_width)
    tok_index = recv_index.reshape(local_pages, row_total)
    tok_weight = jnp.broadcast_to(
        recv_weight[:, :, None], (local_pages, bucket_span, tok_count)
    ).reshape(local_pages, row_total)
    patch_ids = jnp.arange(patch_count, dtype=jnp.int32)[None, :, None]

    def add_block(counter, summed):
        offset = counter * block_rows
        index_part = lax.dynamic_slice_in_dim(tok_index, offset, block_rows, 1)
        weight_part = lax.dynamic_slice_in_dim(tok_weight, offset, block_rows, 1)
        query_part = lax.dynamic_slice_in_dim(tok_query, offset, block_rows, 1)
        one_hot = jnp.where(
            patch_ids == index_part[:, None, :],
            weight_part[:, None, :],
            jnp.zeros((), jnp.bfloat16),
        )
        return summed + jnp.einsum(
            "kpr,krd->kpd", one_hot, query_part, preferred_element_type=jnp.float32
        )

    grad_local = lax.fori_loop(
        0,
        row_total // block_rows,
        add_block,
        jnp.zeros((local_pages, patch_count, embed_width), jnp.float32),
    )
    grad_unit_embed = lax.psum(
        grad_local.reshape(local_pages * patch_count, embed_width), "queries"
    )
    grad_embed = (
        (
            grad_unit_embed
            - unit_embed32 * jnp.sum(unit_embed32 * grad_unit_embed, axis=-1, keepdims=True)
        )
        * inv_embed
    ).astype(jnp.bfloat16)
    grad_part = jnp.einsum("rh,rd->hd", flat_states, grad_embed, preferred_element_type=jnp.float32)
    grad_projection = lax.psum(grad_part, "pages")
    return (grad_queries, grad_projection)


def solution(mesh):
    placed = (
        P("pages", None, "queries"),
        P("queries", None),
        P(("pages", "queries"), None, None),
        P(("pages", "queries"), None),
        P(("pages", "queries"), None, None),
        P(("pages", "queries"), None),
        P(),
    )
    return jax.shard_map(
        body,
        mesh=mesh,
        in_specs=placed,
        out_specs=(P(("pages", "queries"), None, None), P("queries", None)),
        check_vma=False,
    )
```

profile of v0, /device:TPU:1, one launch (start us, length us, event | category | flops | bytes accessed | tf_op | source)
XLA Modules:
  0.0 994.9 jit_solution(18157480221952070199)
XLA Ops:
  7.2 0.7 all-gather.2.cloned.1.call-update
  7.9 0.8 eq.77
  8.7 0.9 select_reduce_fusion
  9.7 0.2 fusion.29
  10.0 0.2 fusion.31
  10.2 1.6 scatter_custom_fusion
  11.8 0.2 copy.75
  12.0 0.9 reshape.248
  12.9 20.4 %all-to-all-start = ((s32[128,1,128]{2,1,0:T(1,128)}), s32[128,1,128]{2,1,0:T(1,128)S(1)}, u32[]{:S(2)}, u32[]{:S(2)}) async-start(s32[128,1,128]{2,1,0:T(1,128)} %reshape.248), calls=%async_computation | async-start | bytes 131072 | tf_op jit(solution)/shard_map/all_to_all | solution.py:65
  33.3 13.2 %all_gather.7 = bf16[128,1536]{0,1:T(8,128)(2,1)S(1)} all-gather(bf16[128,384]{0,1:T(8,128)(2,1)S(1)} %bitcast.65), channel_id=1, replica_groups=mesh['pages'=128,'queries'=4] {'queries'}, dimensions={1}, use_global_device_ids=true | all-gather | bytes 491520 | tf_op jit(solution)/shard_map/all_gather | solution.py:27
  46.5 1.8 all-to-all-done
  48.3 0.5 broadcast.180
  48.8 0.8 reduce
  49.6 0.2 reshape.249
  49.9 0.4 compare_and_fusion
  50.4 28.5 %all-gather.2.cloned.1.call-done = bf16[1536,1536]{1,0:T(8,128)(2,1)} async-done(((bf16[1536,384]{1,0:T(8,128)(2,1)}), bf16[1536,1536]{1,0:T(8,128)(2,1)}) %all-gather.2.cloned.1.call-update) | async-done | bytes 4718608 | tf_op jit(solution)/shard_map/all_gather | solution.py:26
  78.9 4.0 multiply_reduce_fusion.1
  83.0 0.2 copy.47
  83.3 57.4 %gather_fusion = bf16[16384,128]{1,0:T(8,128)(2,1)} fusion(bf16[1536,128]{1,0:T(8,128)(2,1)S(1)} %copy.47, s32[16384]{0:T(1024)S(1)} %broadcast_clamp_fusion), kind=kCustom, calls=%fused_computation | custom fusion | bytes 8454144 | tf_op jit(solution)/shard_map/jit(_take)/gather | solution.py:68
  140.6 9.6 copy_select_fusion
  150.3 17.2 %all-to-all-start.1 = ((bf16[2,256,32,128]{3,2,0,1:T(8,128)(2,1)}), bf16[2,256,32,128]{3,2,0,1:T(8,128)(2,1)}, u32[]{:S(2)}, u32[]{:S(2)}) async-start(bf16[2,256,32,128]{3,2,0,1:T(8,128)(2,1)} %copy_select_fusion), calls=%async_computation.1 | async-start | bytes 8388608 | tf_op jit(solution)/shard_map/all_to_all | solution.py:69
  167.5 0.1 fusion.28
  167.7 0.1 fusion.25
  167.8 0.3 broadcast_in_dim.107
  168.2 2.5 broadcast_in_dim.106
  170.7 26.5 %scatter_fusion = bf16[512,32,128]{2,1,0:T(8,128)(2,1)} fusion(bf16[512,32,128]{2,1,0:T(8,128)(2,1)} %broadcast_in_dim.106, s32[256]{0:T(256)S(1)} %bitcast.73, bf16[256,32,128]{2,1,0:T(8,128)(2,1)S(1)} %bitcast.54), kind=kCustom, calls=%fused_computation.4 | custom fusion | bytes 6292480 | tf_op jit(solution)/shard_map/scatter | solution.py:54
  197.1 5.7 copy.53
  202.8 150.0 %all-to-all-done.1 = bf16[2,256,32,128]{3,2,0,1:T(8,128)(2,1)} async-done(((bf16[2,256,32,128]{3,2,0,1:T(8,128)(2,1)}), bf16[2,256,32,128]{3,2,0,1:T(8,128)(2,1)}, u32[]{:S(2)}, u32[]{:S(2)}) %all-to-all-start.1) | async-done | bytes 4194336 | tf_op jit(solution)/shard_map/all_to_all | solution.py:69
  352.8 12.6 %all-to-all-start.3 = ((bf16[2,256,32,128]{3,2,0,1:T(8,128)(2,1)}), bf16[2,256,32,128]{3,2,0,1:T(8,128)(2,1)}, u32[]{:S(2)}, u32[]{:S(2)}) async-start(bf16[2,256,32,128]{3,2,0,1:T(8,128)(2,1)} %copy.53), calls=%async_computation.3 | async-start | bytes 8388608 | tf_op jit(solution)/shard_map/all_to_all | solution.py:64
  365.4 0.1 fusion.48
  365.5 4.9 copy.49
  370.4 3.2 gather_fusion.1
  373.6 1.1 fusion.17
  374.8 0.1 exponential_reduce_fusion
  375.1 0.5 copy-done.2
  375.6 2.2 scatter_custom_fusion.1
  377.7 0.2 all_to_all.17
  377.9 0.7 copy.51
  378.6 172.0 %all-to-all-done.3 = bf16[2,256,32,128]{3,2,0,1:T(8,128)(2,1)} async-done(((bf16[2,256,32,128]{3,2,0,1:T(8,128)(2,1)}), bf16[2,256,32,128]{3,2,0,1:T(8,128)(2,1)}, u32[]{:S(2)}, u32[]{:S(2)}) %all-to-all-start.3) | async-done | bytes 4194336 | tf_op jit(solution)/shard_map/all_to_all | solution.py:64
  550.6 12.6 %all-to-all-start.2 = ((bf16[2,128,2]{2,0,1:T(2,128)(2,1)}), bf16[2,128,2]{2,0,1:T(2,128)(2,1)}, u32[]{:S(2)}, u32[]{:S(2)}) async-start(bf16[2,128,2]{2,0,1:T(2,128)(2,1)} %copy.51), calls=%async_computation.2 | async-start | bytes 131072 | tf_op jit(solution)/shard_map/all_to_all | solution.py:91
  563.3 0.2 reshape.191
  563.5 4.9 copy.54
  568.4 9.5 all-to-all-done.2
  577.9 0.8 copy.52
  578.7 0.1 broadcast_in_dim.104
  578.9 0.1 broadcast_in_dim.105
  579.0 0.2 reshape.193
  579.2 25.7 %while.14 = (s32[]{:T(128)}, f32[2,768,128]{2,1,0:T(8,128)}, s32[2,8192]{1,0:T(2,128)S(1)}, bf16[2,8192]{1,0:T(2,128)(2,1)S(1)}, bf16[2,8192,128]{2,1,0:T(8,128)...) while((s32[]{:T(128)}, f32[2,768,128]{2,1,0:T(8,128)}, s32[2,8192]{1,0:T(2,128)S(1)}, ...), condition=%wide.region_13.14_spmd.clone, body=%wide.region_12.13_spmd.clone.sunk | while | flops 406192128 | bytes 2134185 | solution.py:121
  579.3 3.0 fusion.54
  582.2 3.2 fusion.54
  585.5 3.2 fusion.54
  588.7 3.2 fusion.54
  592.0 3.2 fusion.54
  595.2 3.2 fusion.54
  598.5 3.2 fusion.54
  601.7 3.2 fusion.54
  604.9 2.3 copy.64
  607.3 0.7 fusion.15
  608.0 47.8 %all-reduce.3.cloned.1.call-done = f32[1536,128]{0,1:T(8,128)} async-done(((f32[1536,128]{0,1:T(8,128)}), f32[1536,128]{0,1:T(8,128)}) %all-reduce.3.cloned.1.call-update) | async-done | bytes 786448 | tf_op jit(solution)/shard_map/psum | solution.py:127
  655.8 1.2 multiply_reduce_fusion
  657.1 2.6 convolution_bitcast_fusion
  659.6 3.2 fusion.21
  662.9 323.8 %all-reduce.5.cloned.1.call-done = f32[384,128]{0,1:T(8,128)} async-done(((f32[384,128]{0,1:T(8,128)}), f32[384,128]{0,1:T(8,128)}) %all-reduce.5.cloned.1.call-update) | async-done | bytes 196624 | tf_op jit(solution)/shard_map/psum | solution.py:138
  986.7 1.7 copy.56
  (50 shorter events, 0.9 us)
Async XLA Ops:
  7.2 26.2 %copy-start.1 = (bf16[384,128]{1,0:T(8,128)(2,1)S(1)}, bf16[384,128]{1,0:T(8,128)(2,1)}, u32[]{:S(2)}) copy-start(bf16[384,128]{1,0:T(8,128)(2,1)} %param.10) | copy-start | bytes 294916
  7.2 71.7 %all-gather.2.cloned.1.call-start = ((), (), s32[]{:S(2)}) async-start(), calls=%async_computation.4 | async-start | bytes 5898240 | tf_op jit(solution)/shard_map/all_gather | solution.py:26
  12.9 35.4 %all-to-all-start = ((s32[128,1,128]{2,1,0:T(1,128)}), s32[128,1,128]{2,1,0:T(1,128)S(1)}, u32[]{:S(2)}, u32[]{:S(2)}) async-start(s32[128,1,128]{2,1,0:T(1,128)} %reshape.248), calls=%async_computation | async-start | bytes 131072 | tf_op jit(solution)/shard_map/all_to_all | solution.py:65
  150.3 17.3 %copy-start = (bf16[16,32,128]{2,1,0:T(8,128)(2,1)S(1)}, bf16[16,32,128]{2,1,0:T(8,128)(2,1)}, u32[]{:S(2)}) copy-start(bf16[16,32,128]{2,1,0:T(8,128)(2,1)} %param.11) | copy-start | bytes 393220
  150.3 202.5 %all-to-all-start.1 = ((bf16[2,256,32,128]{3,2,0,1:T(8,128)(2,1)}), bf16[2,256,32,128]{3,2,0,1:T(8,128)(2,1)}, u32[]{:S(2)}, u32[]{:S(2)}) async-start(bf16[2,256,32,128]{3,2,0,1:T(8,128)(2,1)} %copy_select_fusion), calls=%async_computation.1 | async-start | bytes 8388608 | tf_op jit(solution)/shard_map/all_to_all | solution.py:69
  352.8 197.9 %all-to-all-start.3 = ((bf16[2,256,32,128]{3,2,0,1:T(8,128)(2,1)}), bf16[2,256,32,128]{3,2,0,1:T(8,128)(2,1)}, u32[]{:S(2)}, u32[]{:S(2)}) async-start(bf16[2,256,32,128]{3,2,0,1:T(8,128)(2,1)} %copy.53), calls=%async_computation.3 | async-start | bytes 8388608 | tf_op jit(solution)/shard_map/all_to_all | solution.py:64
  370.4 4.3 copy-start.4
  375.0 0.6 copy-start.2
  550.6 27.2 %all-to-all-start.2 = ((bf16[2,128,2]{2,0,1:T(2,128)(2,1)}), bf16[2,128,2]{2,0,1:T(2,128)(2,1)}, u32[]{:S(2)}, u32[]{:S(2)}) async-start(bf16[2,128,2]{2,0,1:T(2,128)(2,1)} %copy.51), calls=%async_computation.2 | async-start | bytes 131072 | tf_op jit(solution)/shard_map/all_to_all | solution.py:91
  563.2 92.6 %all-reduce.3.cloned.1.call-start = ((), (), s32[]{:S(2)}) async-start(), calls=%async_computation.5 | async-start | bytes 1572864 | tf_op jit(solution)/shard_map/psum | solution.py:127
  579.2 28.1 %copy-start.3 = (bf16[16,16]{1,0:T(8,128)(2,1)S(1)}, bf16[16,16]{1,0:T(8,128)(2,1)}, u32[]{:S(2)}) copy-start(bf16[16,16]{1,0:T(8,128)(2,1)} %copy-done.2) | copy-start | bytes 1540
  607.2 379.4 %all-reduce.5.cloned.1.call-start = ((), (), s32[]{:S(2)}) async-start(), calls=%async_computation.6 | async-start | bytes 393216 | tf_op jit(solution)/shard_map/psum | solution.py:138
Sparse Core Ops, SparseCore 0:
  10.1 68.7 all-gather.1
  607.4 48.4 all-reduce.2
  659.9 326.7 all-reduce.4
where the time goes:
time: 998 us; the launch traced here: 995 us
  waiting for transfers between devices  734 us (74%)
  local copies, waits for them, and re-layouts  119 us (12%)
  starting transfers between devices  62.9 us (6%)
  matrix products  34 us (3%)
  other arithmetic  17.3 us (2%)
  between operations  14.1 us (1%)
  blocking collectives  13.2 us (1%)
    psum x1, waiting for transfers between devices, body(): grad_projection = lax.psum(grad_part, 'pages')  324 us
    all_to_all x1, waiting for transfers between devices, body(): lax.all_to_all(send_query, 'pages', split_axis=1, concat_axis=1, tiled=True)  172 us
    all_to_all x1, waiting for transfers between devices, body(): lax.all_to_all(picked, 'pages', split_axis=1, concat_axis=1, tiled=True)  150 us
    gather x1, local copies, waits for them, and re-layouts, body(): picked = jnp.take(unit_embed, recv_index + page_base, axis=0)  57.4 us
    psum x1, waiting for transfers between devices, body(): lax.psum(grad_local.reshape(local_pages * patch_count, embed_width), 'que...  47.8 us
    all_gather x1, waiting for transfers between devices, body(): lax.all_gather(flat_states, 'queries', axis=1, tiled=True)  28.5 us
    scatter x1, local copies, waits for them, and re-layouts, body(): send_query = jnp.zeros((slot_total, tok_count, embed_width), jnp.bfloat16...  26.5 us
    dot_general x8, matrix products, add_block(): jnp.einsum('kpr,krd->kpd', one_hot, query_part, preferred_element_type=jn...  25.6 us
  transfers between devices with their start and end apart: 7, of which 7 were waited for; matrix products, arithmetic and copies ran while one was open for 6% of the time, Pallas kernels for 0%

commit v1 on v0

v1 whole, which is shorter than its diff:
```python
import functools

import jax
import jax.numpy as jnp
from jax import lax
from jax.experimental import pallas as pl
from jax.experimental.pallas import tpu as pltpu
from jax.sharding import PartitionSpec as P

SOFTMAX_HEAT = 0.5
EPSILON = 1e-06
CAP = 2
X = 4
MESH = pl.DeviceIdType.MESH
VMEM = pl.BlockSpec(memory_space=pltpu.VMEM)
SUBS = 2


def unit_rows(values):
    inverse = lax.rsqrt(jnp.sum(values * values, axis=-1, keepdims=True) + EPSILON)
    return (values * inverse, inverse)


def place(zs):
    p = lax.axis_index("pages")
    return p // (2 * zs), lax.axis_index("queries"), (p // 2) % zs, p % 2


def dev(zs, x, y, z, c):
    return ((x * zs + z) * 2 + c, y)


def remote(src, dst, send, recv, to):
    return pltpu.make_async_remote_copy(
        src_ref=src, dst_ref=dst, send_sem=send, recv_sem=recv, device_id=to, device_id_type=MESH
    )


def greet(barrier, devices):
    for to in devices:
        pl.semaphore_signal(barrier, inc=1, device_id=to, device_id_type=MESH)
    pl.semaphore_wait(barrier, len(devices))


def gather_kernel(
    zs, ys, q, idx, nt, ep, qall, idxall, ntall, table, ef, rs,
    q_s, q_r, e_s, e_r, t_s, t_r, f_s, f_r, i_s, i_r, n_s, n_r,
):
    x, y, z, c = place(zs)
    at = functools.partial(dev, zs)
    rows = ef.shape[0]
    part = q.shape[0] // SUBS
    half = zs // 2
    plane = [(dx, dy) for dx in range(X) for dy in range(ys) if dx + dy > 0]
    greet(
        pltpu.get_barrier_semaphore(),
        [at(x, y, (z + d) % zs, c) for d in range(1, zs)]
        + [at((x + dx) % X, (y + dy) % ys, z, c) for dx, dy in plane]
        + [at(x, y, z, 1 - c)],
    )
    qall[z] = q[...]

    def ring(way, s, h, block):
        ref = qall.at[block, pl.ds(h * part, part)]
        k = 0 if way > 0 else 1
        return remote(ref, ref, q_s.at[k, s, h], q_r.at[k, s, h], at(x, y, (z + way + zs) % zs, c))

    def ring_parts(way, s):
        if s < half - 1:
            return range(SUBS)
        return range(SUBS // 2) if way > 0 else range(SUBS // 2, SUBS)

    def ring_send(s):
        for h in range(SUBS):
            for way in (1, -1):
                block = (z - way * s + zs) % zs
                if s > 0:
                    ring(way, s - 1, h, block).wait_recv()
                if h in ring_parts(way, s):
                    ring(way, s, h, block).start()

    ring_send(0)
    e_copies = []
    for d in range(1, ys):
        yd = (y + d) % ys
        src = ep.at[pl.ds(pl.multiple_of(yd * rows, 8), rows)]
        e_copies.append(remote(src, rs.at[d - 1], e_s.at[d - 1], e_r.at[d - 1], at(x, yd, z, c)))
        e_copies[-1].start()
    i_copies = []
    for d in range(1, zs):
        zd = (z + d) % zs
        to = at(x, y, zd, c)
        i_copies.append(remote(idx.at[zd], idxall.at[z], i_s.at[d - 1], i_r.at[d - 1], to))
        i_copies.append(remote(nt.at[zd], ntall.at[z], n_s.at[d - 1], n_r.at[d - 1], to))
        i_copies[-2].start()
        i_copies[-1].start()
    idxall[z] = idx[z]
    ntall[z] = nt[z]
    ring_send(1)
    ring_send(2)

    for copy in e_copies:
        copy.wait_recv()
    own = ep[pl.ds(pl.multiple_of(y * rows, 8), rows), :]
    for d in range(1, ys):
        own = own + rs[d - 1]
    ef[...] = own
    table[x, c, y] = unit_rows(own)[0].astype(jnp.bfloat16)
    t_copies = []
    mine = table.at[x, c, y]
    for i, (dx, dy) in enumerate(plane):
        to = at((x + dx) % X, (y + dy) % ys, z, c)
        t_copies.append(remote(mine, mine, t_s.at[i], t_r.at[i], to))
        t_copies[-1].start()
    f_copies = []

    def forward(i, xx, yy):
        ref = table.at[xx, c, yy]
        f_copies.append(remote(ref, ref, f_s.at[i], f_r.at[i], at(x, y, z, 1 - c)))
        f_copies[-1].start()

    forward(len(plane), x, y)
    s = 3
    for i, (dx, dy) in enumerate(plane):
        if i % 3 == 0 and s < half:
            ring_send(s)
            s += 1
        t_copies[i].wait_recv()
        forward(i, (x - dx + X) % X, (y - dy + ys) % ys)
    while s < half:
        ring_send(s)
        s += 1
    for way in (1, -1):
        for h in ring_parts(way, half - 1):
            ring(way, half - 1, h, (z - way * half + zs) % zs).wait_recv()
    for copy in f_copies + i_copies:
        copy.wait_recv()
    for s in range(half):
        for way in (1, -1):
            for h in ring_parts(way, s):
                ring(way, s, h, (z - way * s + zs) % zs).wait_send()
    for copy in e_copies + i_copies + t_copies + f_copies:
        copy.wait_send()


def pick_kernel(n_ref, table, idxt, qall, picked, scored):
    m = pl.program_id(0)
    toks, slots = idxt.shape[1:]
    rows = table.shape[1]
    lanes = lax.broadcasted_iota(jnp.int32, (toks, rows), 1)
    group = 8
    page = table[0]
    ids = idxt[0]
    for g in range(slots // group):
        hot = jnp.concatenate(
            [
                jnp.where(ids[:, s : s + 1] == lanes, 1.0, 0.0).astype(jnp.bfloat16)
                for s in range(g * group, (g + 1) * group)
            ],
            axis=0,
        )
        got = jnp.dot(hot, page, preferred_element_type=jnp.float32)
        picked[0, g * group * toks : (g + 1) * group * toks, :] = got.astype(jnp.bfloat16)
        for i in range(group):
            s = g * group + i
            query = qall[n_ref[m * slots + s]].astype(jnp.float32)
            scored[0, s : s + 1, :] = jnp.sum(
                got[i * toks : (i + 1) * toks] * query, axis=0, keepdims=True
            )


def total_kernel(zs, part, total, seen, s_s, s_r):
    x, y, z, c = place(zs)
    peers = [dev(zs, x, y, (z + d) % zs, c) for d in range(1, zs)]
    greet(pltpu.get_barrier_semaphore(), peers)
    copies = [
        remote(part, seen.at[i], s_s.at[i], s_r.at[i], to) for i, to in enumerate(peers)
    ]
    for copy in copies:
        copy.start()
    out = part[...]
    for i, copy in enumerate(copies):
        copy.wait_recv()
        out = out + seen[i]
    total[...] = out
    for copy in copies:
        copy.wait_send()


def spread_kernel(n_ref, w_ref, picked, idxl, wl, qall, gq, ge, qsel):
    m = pl.program_id(0)
    slots = n_ref.shape[0] // pl.num_programs(0)
    toks = qall.shape[1]
    rows = ge.shape[1]

    @pl.when(m == 0)
    def _():
        gq[...] = jnp.zeros_like(gq)

    for s in range(slots):
        n = n_ref[m * slots + s]
        qsel[s * toks : (s + 1) * toks, :] = qall[n]
        rows_of = picked[0, s * toks : (s + 1) * toks, :].astype(jnp.float32)
        gq[n] = gq[n] + w_ref[m * slots + s] * rows_of
    total = slots * toks
    width = 256
    ids = lax.broadcasted_iota(jnp.int32, (rows, width), 0)
    out = jnp.zeros((rows, qall.shape[2]), jnp.float32)
    for k in range(total // width):
        cut = slice(k * width, (k + 1) * width)
        hot = jnp.where(idxl[0, :, cut] == ids, wl[0, :, cut], 0.0).astype(jnp.bfloat16)
        out = out + jnp.dot(hot, qsel[cut, :], preferred_element_type=jnp.float32)
    ge[0] = out


def reduce_kernel(
    zs, ys, gq, ge, ef, gout, eout, rbuf, cbuf, sbuf, xbuf,
    g_s, g_r, c_s, c_r, t_s, t_r, y_s, y_r,
):
    x, y, z, c = place(zs)
    at = functools.partial(dev, zs)
    half = zs // 2
    part = gout.shape[0] // 2
    rows = ef.shape[0]
    plane = [(dx, dy) for dx in range(X) for dy in range(ys) if dx + dy > 0]
    greet(
        pltpu.get_barrier_semaphore(),
        [at(x, y, (z + 1) % zs, c), at(x, y, (z + zs - 1) % zs, c)]
        + [at((x + dx) % X, (y + dy) % ys, z, c) for dx, dy in plane]
        + [at(x, y, z, 1 - c)],
    )

    def first(way, h):
        return 0 if (h == 0) == (way > 0) else 1

    def ring(way, s, h):
        k = 0 if way > 0 else 1
        block = (z + way * (half - s) + zs) % zs
        cut = pl.ds(h * part, part)
        src = gq.at[block, cut] if s == first(way, h) else rbuf.at[k, s - 1, cut]
        return remote(
            src, rbuf.at[k, s, cut], g_s.at[k, s, h], g_r.at[k, s, h],
            at(x, y, (z + way + zs) % zs, c),
        )

    def ring_step(s):
        for h in range(2):
            for way in (1, -1):
                k = 0 if way > 0 else 1
                start = first(way, h)
                if s < start:
                    continue
                if s > start:
                    ring(way, s - 1, h).wait_recv()
                    block = (z + way * (half - s) + zs) % zs
                    cut = pl.ds(h * part, part)
                    rbuf[k, s - 1, cut] = rbuf[k, s - 1, cut] + gq[block, cut]
                ring(way, s, h).start()

    ring_step(0)
    c_copies = []
    for dx in range(X):
        xx = (x + dx) % X
        c_copies.append(
            remote(ge.at[xx, 1 - c], cbuf.at[xx], c_s.at[dx], c_r.at[dx], at(x, y, z, 1 - c))
        )
    for dx in list(range(1, X)) + [0]:
        c_copies[dx].start()
    ring_step(1)
    t_copies = {}
    for dx in list(range(1, X)) + [0]:
        xx = (x + dx) % X
        c_copies[dx].wait_recv()
        for dy in range(ys):
            yy = (y + dy) % ys
            cut = pl.ds(pl.multiple_of(yy * rows, 8), rows)
            both = ge[xx, c, cut] + cbuf[xx, cut]
            if dx + dy == 0:
                own = both
                continue
            i = plane.index((dx, dy))
            sbuf[i] = both.astype(jnp.bfloat16)
            to = at(xx, yy, z, c)
            t_copies[i] = remote(sbuf.at[i], xbuf.at[i], t_s.at[i], t_r.at[i], to)
            t_copies[i].start()
    ring_step(2)
    ring_step(3)
    ring_step(4)
    for i in range(len(plane)):
        t_copies[i].wait_recv()
        own = own + xbuf[i].astype(jnp.float32)
    unit, inverse = unit_rows(ef[...])
    grad = (own - unit * jnp.sum(unit * own, axis=-1, keepdims=True)) * inverse
    eout[y] = grad.astype(jnp.bfloat16)
    y_copies = []
    for d in range(1, ys):
        y_copies.append(
            remote(
                eout.at[y], eout.at[y], y_s.at[d - 1], y_r.at[d - 1], at(x, (y + d) % ys, z, c)
            )
        )
        y_copies[-1].start()
    for s in range(5, half):
        ring_step(s)
    out = gq[z]
    for k, way in ((0, 1), (1, -1)):
        for h in range(2):
            ring(way, half - 1, h).wait_recv()
        out = out + rbuf[k, half - 1]
    gout[...] = out
    for copy in y_copies:
        copy.wait_recv()
    for s in range(half):
        for way in (1, -1):
            for h in range(2):
                if s >= first(way, h):
                    ring(way, s, h).wait_send()
    for copy in c_copies + list(t_copies.values()) + y_copies:
        copy.wait_send()


def sum_kernel(
    zs, part, out, abuf, bsrc, bbuf, a_s, a_r, b_s, b_r, c_s, c_r, d_s, d_r
):
    x, y, z, c = place(zs)
    at = functools.partial(dev, zs)
    rows = part.shape[0] // (2 * X)
    owners = rows // 8
    plane = [(dx, dc) for dx in range(X) for dc in range(2) if dx + dc > 0]
    near = [at((x + dx) % X, y, z, (c + dc) % 2) for dx, dc in plane]
    far = [at(x, y, (z + d) % zs, c) for d in range(1, zs)]
    greet(pltpu.get_barrier_semaphore(), near + far)
    me = x * 2 + c

    def block(k):
        return pl.ds(pl.multiple_of(k * rows, 8), rows)

    a_copies = []
    for i, (dx, dc) in enumerate(plane):
        k = ((x + dx) % X) * 2 + (c + dc) % 2
        a_copies.append(remote(part.at[block(k)], abuf.at[i], a_s.at[i], a_r.at[i], near[i]))
        a_copies[-1].start()
    own = part[block(me), :]
    for i, copy in enumerate(a_copies):
        copy.wait_recv()
        own = own + abuf[i]
    bsrc[...] = own

    def tile(k):
        return pl.ds(pl.multiple_of(k * 8, 8), 8)

    def b_copy(k, i, to):
        return remote(bsrc.at[tile(k)], bbuf.at[i], b_s.at[k], b_r.at[i], to)

    for k in range(owners):
        @pl.when(z != k)
        def _():
            b_copy(k, z, at(x, y, k, c)).start()

    my_tile = pl.ds(pl.multiple_of(me * rows + z * 8, 8), 8)

    def c_copy(i, zd):
        return remote(out.at[my_tile], out.at[my_tile], c_s.at[i], c_r.at[z], at(x, y, zd, c))

    @pl.when(z < owners)
    def _():
        total = bsrc[tile(z), :]
        for d in range(1, zs):
            i = (z + d) % zs
            b_copy(0, i, at(x, y, i, c)).wait_recv()
            total = total + bbuf[i]
        out[my_tile, :] = total
        for d in range(1, zs):
            c_copy(d - 1, (z + d) % zs).start()

    for k in range(owners):
        @pl.when(z != k)
        def _():
            got = out.at[pl.ds(pl.multiple_of(me * rows + k * 8, 8), 8)]
            remote(got, got, c_s.at[0], c_r.at[k], at(x, y, k, c)).wait_recv()

    d_copies = []
    for i in range(len(plane)):
        ref = out.at[block(me)]
        d_copies.append(remote(ref, ref, d_s.at[i], d_r.at[i], near[i]))
        d_copies[-1].start()
    for copy in d_copies:
        copy.wait_recv()
    for copy in a_copies + d_copies:
        copy.wait_send()
    for k in range(owners):
        @pl.when(z != k)
        def _():
            b_copy(k, z, at(x, y, k, c)).wait_send()

    @pl.when(z < owners)
    def _():
        for d in range(1, zs):
            c_copy(d - 1, (z + d) % zs).wait_send()


def dma(*shape):
    return pltpu.SemaphoreType.DMA(shape)


def talk(number):
    return pltpu.CompilerParams(
        collective_id=number, has_side_effects=True, vmem_limit_bytes=48 << 20
    )


def body(page_states, projection, query_tokens, candidates, patch_index, teacher_logits, page_slot):
    ys = lax.axis_size("queries")
    zs = lax.axis_size("pages") // (2 * X)
    held, patches, share = page_states.shape
    width = projection.shape[1]
    nq, nc, toks = patch_index.shape
    pages = page_slot.shape[0]
    pairs = nq * nc
    chip = 2 * held
    slab = X * chip
    slots = slab * CAP
    rows = held * patches // ys
    f32, bf16, i32 = jnp.float32, jnp.bfloat16, jnp.int32
    S = jax.ShapeDtypeStruct
    plane = X * ys - 1
    half = zs // 2

    states = page_states.reshape(held * patches, share)
    partial = jnp.dot(states, projection, preferred_element_type=f32)
    unit_query32, inv_query = unit_rows(query_tokens.astype(f32))
    unit_query = unit_query32.astype(bf16)

    flat = candidates.reshape(pairs)
    ids = jnp.arange(pages, dtype=i32)
    row = jnp.sum(jnp.where(flat[:, None] == ids[None, :], page_slot[None, :], 0), axis=1)
    before = jnp.arange(pairs)[None, :] < jnp.arange(pairs)[:, None]
    arrival = jnp.sum(((row[:, None] == row[None, :]) & before).astype(i32), axis=1)
    target = (
        ((row // chip) % zs * slab + row // (chip * zs) * chip + row % chip) * CAP + arrival
    )
    hot = target[None, :] == jnp.arange(zs * slots, dtype=i32)[:, None]
    number = jnp.sum(jnp.where(hot, jnp.arange(pairs, dtype=i32)[None, :] // nc + 1, 0), axis=1) - 1
    probs = jnp.exp(teacher_logits)
    probs = probs / jnp.sum(probs, axis=1, keepdims=True)
    teach = jnp.sum(jnp.where(hot, probs.reshape(1, pairs), 0.0), axis=1)
    flat_index = patch_index.reshape(pairs, toks)
    digits = jnp.concatenate([flat_index // 32, flat_index % 32], axis=1).astype(bf16)
    digits = jnp.dot(hot.astype(bf16), digits, preferred_element_type=f32)
    index = (digits[:, :toks] * 32 + digits[:, toks:]).astype(i32)
    index = jnp.where(number[:, None] >= 0, index, -1)
    index = index.reshape(zs, slots * toks // 128, 128)
    nt = jnp.concatenate(
        [
            number.astype(f32).reshape(zs, slots),
            teach.reshape(zs, slots),
            jnp.zeros((zs, 128 - 2 * slots), f32),
        ],
        axis=1,
    ).reshape(zs, 1, 128)

    qall, idxall, ntall, table, ef = pl.pallas_call(
        functools.partial(gather_kernel, zs, ys),
        out_shape=(
            S((zs, nq * toks, width), bf16),
            S(index.shape, i32),
            S(nt.shape, f32),
            S((X, 2, ys, rows, width), bf16),
            S((rows, width), f32),
        ),
        in_specs=[VMEM] * 4,
        out_specs=(VMEM,) * 5,
        scratch_shapes=[
            pltpu.VMEM((ys - 1, rows, width), f32),
            dma(2, half, SUBS), dma(2, half, SUBS),
            dma(ys - 1), dma(ys - 1),
            dma(plane), dma(plane),
            dma(plane + 1), dma(plane + 1),
            dma(zs - 1), dma(zs - 1),
            dma(zs - 1), dma(zs - 1),
        ],
        compiler_params=talk(0),
        name="gather",
    )(unit_query.reshape(nq * toks, width), index, nt, partial)

    per_page = zs * CAP
    idx4 = idxall.reshape(zs, slab, CAP, toks)
    idxt = idx4.transpose(1, 3, 0, 2).reshape(slab, toks, per_page)
    idxl = idx4.transpose(1, 0, 2, 3).reshape(slab, 1, per_page * toks)
    num = ntall[:, 0, :slots].astype(i32).reshape(zs, slab, CAP).transpose(1, 0, 2)
    teach = ntall[:, 0, slots : 2 * slots].reshape(zs, slab, CAP).transpose(1, 0, 2)
    valid = num >= 0
    where = jnp.maximum(num, 0) + nq * jnp.arange(zs, dtype=i32)[None, :, None]
    where = where.reshape(slab * per_page)
    qall = qall.reshape(zs * nq, toks, width)
    table = table.reshape(slab, patches, width)
    whole = pl.BlockSpec((zs * nq, toks, width), lambda m, *_: (0, 0, 0))

    def one(*shape):
        return pl.BlockSpec((1,) + shape, lambda m, *_: (m, 0, 0))

    picked, scored = pl.pallas_call(
        pick_kernel,
        out_shape=(S((slab, per_page * toks, width), bf16), S((slab, per_page, width), f32)),
        grid_spec=pltpu.PrefetchScalarGridSpec(
            num_scalar_prefetch=1,
            grid=(slab,),
            in_specs=[one(patches, width), one(toks, per_page), whole],
            out_specs=(one(per_page * toks, width), one(per_page, width)),
        ),
        compiler_params=pltpu.CompilerParams(vmem_limit_bytes=48 << 20),
        name="pick",
    )(where, table, idxt, qall)

    scores = jnp.sum(scored, axis=-1).reshape(slab, zs, CAP)
    lifted = jnp.where(valid, jnp.exp(scores / SOFTMAX_HEAT), 0.0)
    is_n = num[..., None] == jnp.arange(nq, dtype=i32)
    part = jnp.sum(jnp.where(is_n, lifted[..., None], 0.0), axis=(0, 2))
    total = pl.pallas_call(
        functools.partial(total_kernel, zs),
        out_shape=S((zs * nq // 128, 128), f32),
        in_specs=[VMEM],
        out_specs=VMEM,
        scratch_shapes=[
            pltpu.VMEM((zs - 1, zs * nq // 128, 128), f32), dma(zs - 1), dma(zs - 1),
        ],
        compiler_params=talk(1),
        name="total",
    )(part.reshape(zs * nq // 128, 128)).reshape(1, zs, 1, nq)
    mine = jnp.sum(jnp.where(is_n, total, 0.0), axis=-1)
    weight = jnp.where(
        valid, (lifted / jnp.where(valid, mine, 1.0) - teach) / SOFTMAX_HEAT, 0.0
    ).astype(bf16).astype(f32)
    flat_weight = weight.reshape(slab * per_page)
    wide = jnp.broadcast_to(
        weight.reshape(slab, 1, per_page, 1), (slab, 1, per_page, toks)
    ).reshape(slab, 1, per_page * toks)

    gq, ge = pl.pallas_call(
        spread_kernel,
        out_shape=(S((zs * nq, toks, width), f32), S((slab, patches, width), f32)),
        grid_spec=pltpu.PrefetchScalarGridSpec(
            num_scalar_prefetch=2,
            grid=(slab,),
            in_specs=[
                one(per_page * toks, width), one(1, per_page * toks), one(1, per_page * toks),
                whole,
            ],
            out_specs=(whole, one(patches, width)),
            scratch_shapes=[pltpu.VMEM((per_page * toks, width), bf16)],
        ),
        compiler_params=pltpu.CompilerParams(vmem_limit_bytes=48 << 20),
        name="spread",
    )(where, flat_weight, picked, idxl, wide, qall)

    gout, eout = pl.pallas_call(
        functools.partial(reduce_kernel, zs, ys),
        out_shape=(S((nq * toks, width), f32), S((ys, rows, width), bf16)),
        in_specs=[VMEM] * 3,
        out_specs=(VMEM,) * 2,
        scratch_shapes=[
            pltpu.VMEM((2, half, nq * toks, width), f32),
            pltpu.VMEM((X, held * patches, width), f32),
            pltpu.VMEM((plane, rows, width), bf16),
            pltpu.VMEM((plane, rows, width), bf16),
            dma(2, half, 2), dma(2, half, 2),
            dma(X), dma(X),
            dma(plane), dma(plane),
            dma(ys - 1), dma(ys - 1),
        ],
        compiler_params=talk(2),
        name="reduce",
    )(gq.reshape(zs, nq * toks, width), ge.reshape(X, 2, held * patches, width), ef)

    grad_unit = gout.reshape(nq, toks, width)
    grad_queries = (
        grad_unit - unit_query32 * jnp.sum(unit_query32 * grad_unit, axis=-1, keepdims=True)
    ) * inv_query
    grad_part = lax.dot_general(
        states, eout.reshape(held * patches, width), (((0,), (0,)), ((), ())),
        preferred_element_type=f32,
    )
    near = 2 * X - 1
    block = share // (2 * X)
    grad_projection = pl.pallas_call(
        functools.partial(sum_kernel, zs),
        out_shape=S((share, width), f32),
        in_specs=[VMEM],
        out_specs=VMEM,
        scratch_shapes=[
            pltpu.VMEM((near, block, width), f32),
            pltpu.VMEM((block, width), f32),
            pltpu.VMEM((zs, 8, width), f32),
            dma(near), dma(near),
            dma(block // 8), dma(zs),
            dma(zs), dma(zs),
            dma(near), dma(near),
        ],
        compiler_params=talk(3),
        name="sum",
    )(grad_part)
    return (grad_queries, grad_projection)


def solution(mesh):
    placed = (
        P("pages", None, "queries"),
        P("queries", None),
        P(("pages", "queries"), None, None),
        P(("pages", "queries"), None),
        P(("pages", "queries"), None, None),
        P(("pages", "queries"), None),
        P(),
    )
    return jax.shard_map(
        body,
        mesh=mesh,
        in_specs=placed,
        out_specs=(P(("pages", "queries"), None, None), P("queries", None)),
        check_vma=False,
    )
```

time: 998 us -> 230 us (0.23)
  waiting for transfers between devices: 734 us -> 0 us
  Pallas kernels: 0 us -> 193 us
  local copies, waits for them, and re-layouts: 119 us -> 19.9 us
  starting transfers between devices: 62.9 us -> 0 us
  matrix products: 34 us -> 1.33 us
  blocking collectives: 13.2 us -> 0 us
  between operations: 14.1 us -> 0.9 us
    psum x2 -> x0, waiting for transfers between devices: 372 us -> none  [the longest x1 324 us: body(): grad_projection = lax.psum(grad_part, 'pages')]
    all_to_all x4 -> x0, waiting for transfers between devices: 333 us -> none  [the longest x1 172 us: body(): lax.all_to_all(send_query, 'pages', split_axis=1, concat_axis=1, tiled=True)]
    pallas_call x0 -> x6, Pallas kernels: none -> 193 us  [the longest x1 61.6 us: body(): pl.pallas_call(functools.partial(reduce_kernel, zs, ys), out_shape=(S((nq...]
    all_to_all x4 -> x0, starting transfers between devices: 62.8 us -> none  [the longest x1 20.4 us: body(): lax.all_to_all(send_index, 'pages', split_axis=1, concat_axis=1, tiled=True)]
    gather x2 -> x0, local copies, waits for them, and re-layouts: 60.6 us -> none  [the longest x1 57.4 us: body(): picked = jnp.take(unit_embed, recv_index + page_base, axis=0)]
    dot_general x12 -> x3, matrix products: 34 us -> 1.33 us  [the longest x1 0.59 us: body(): lax.dot_general(states, eout.reshape(held * patches, width), (((0,), (0,)...]
    scatter x3 -> x0, local copies, waits for them, and re-layouts: 30.2 us -> none  [the longest x1 26.5 us: body(): send_query = jnp.zeros((slot_total, tok_count, embed_width), jnp.bfloat16...]
    all_gather x1 -> x0, waiting for transfers between devices: 28.5 us -> none  [body(): lax.all_gather(flat_states, 'queries', axis=1, tiled=True)]
  transfers between devices with their start and end apart: 7 -> 0, of which waited for: 7 -> 0; matrix products, arithmetic and copies ran while one was open for 6% -> 0% of each run, Pallas kernels for 0% -> 0%
where the time goes in v1:
time: 230 us; the launch traced here: 229 us
  Pallas kernels  193 us (84%)
  local copies, waits for them, and re-layouts  19.9 us (9%)
  other arithmetic  14.1 us (6%)
    pallas_call x1, Pallas kernels, body(): pl.pallas_call(functools.partial(reduce_kernel, zs, ys), out_shape=(S((nq...  61.6 us
    pallas_call x1, Pallas kernels, body(): pl.pallas_call(functools.partial(gather_kernel, zs, ys), out_shape=(S((zs...  57 us
    pallas_call x1, Pallas kernels, body(): pl.pallas_call(functools.partial(sum_kernel, zs), out_shape=S((share, wid...  31.8 us
    pallas_call x1, Pallas kernels, body(): pl.pallas_call(spread_kernel, out_shape=(S((zs * nq, toks, width), f32),...  17.1 us
    pallas_call x1, Pallas kernels, body(): pl.pallas_call(pick_kernel, out_shape=(S((slab, per_page * toks, width),...  13.2 us
    pallas_call x1, Pallas kernels, body(): pl.pallas_call(functools.partial(total_kernel, zs), out_shape=S((zs * nq...  12.3 us
    unnamed x25, local copies, waits for them, and re-layouts  7.42 us

profile of v1, /device:TPU:1, one launch (start us, length us, event | category | flops | bytes accessed | tf_op | source)
XLA Modules:
  0.0 229.1 jit_solution(15287186631146414531)
XLA Ops:
  0.6 0.0 copy-start
  0.7 1.3 copy-done
  1.9 0.8 exponential_reduce_fusion
  2.7 0.1 pad.2.clone
  2.8 0.8 eq.61
  3.6 0.9 select_reduce_fusion.4
  4.4 0.2 convert_reduce_fusion
  4.7 0.2 select_reduce_fusion.1
  4.8 0.1 convert_element_type.39
  4.9 0.8 exponential_divide_fusion
  5.7 0.1 broadcast_in_dim.117
  5.8 0.2 select_reduce_fusion
  5.9 0.1 reshape.205
  6.0 0.1 maximum_maximum_fusion
  6.1 1.1 fusion.9
  7.2 0.0 copy-start.10
  7.2 1.0 fusion.6
  8.2 1.0 fusion.12
  9.3 0.3 fusion.4
  9.6 0.1 copy.57
  9.7 0.1 reshape.204.idx
  9.8 0.5 fusion.31.ep
  10.3 57.0 %gather.1 = (bf16[16,512,128]{2,1,0:T(8,128)(2,1)S(1)}, s32[16,8,128]{2,1,0:T(8,128)S(1)}, f32[16,1,128]{2,1,0:T(1,128)S(1)}, bf16[4,2,4,384,128]{4,3,2,1,0:T(8,128)(2,1)}, f32[384,128]{1,0:T(8,128)S(1)}) custom-call(bf16[512,128]{1,0:T(8,128)(2,1)S(1)} %bitcast.61, s32[16,8,128]{2,1,0:T(8,128)S(1)} %reshape.204.idx, f32[16,1,128]{2,1,0:T(1,128)S(1)} %bitcast.64, ...), custom_call_target="tpu_custom_call" | custom-call | tf_op jit(solution)/shard_map/gather/pallas_call | solution.py:462
  67.3 0.0 copy-start.5
  67.3 0.7 copy-done.5
  68.0 0.1 fusion.30
  68.0 0.7 copy.64
  68.7 0.1 copy.58
  68.8 0.2 copy.59
  69.0 0.1 reshape.208.n_ref
  69.1 1.0 reshape.210
  70.1 1.8 copy.72
  71.9 1.7 copy.60
  73.6 1.1 copy.61.idxt
  74.7 1.8 reshape.215.idxl
  76.5 1.9 copy-done.2
  78.4 13.2 %pick.1 = (bf16[16,1024,128]{2,1,0:T(8,128)(2,1)}, f32[16,32,128]{2,1,0:T(8,128)S(1)}) custom-call(s32[512]{0:T(512)S(1)} %reshape.208.n_ref, bf16[16,768,128]{2,1,0:T(8,128)(2,1)S(1)} %bitcast.60, s32[16,32,32]{2,1,0:T(8,128)S(1)} %copy.61.idxt, bf16[256,32,128]{2,1,0:T(8,128)(2,1)S(1)} %bitcast.57), custom_call_target="tpu_custom_call" | custom-call | tf_op jit(solution)/shard_map/pick/pallas_call | solution.py:502
  91.6 0.7 copy-done.4
  92.3 1.1 reduce_sum.96
  93.4 0.1 copy.62
  93.5 0.1 copy.63
  93.6 0.7 broadcast_select_fusion
  94.3 0.9 select_reduce_fusion.3
  95.2 0.1 reshape.213.part
  95.3 12.3 %total.1 = f32[2,128]{1,0:T(2,128)S(1)} custom-call(f32[2,128]{1,0:T(2,128)S(1)} %reshape.213.part), custom_call_target="tpu_custom_call" | custom-call | tf_op jit(solution)/shard_map/total/pallas_call | solution.py:519
  107.6 0.1 broadcast_in_dim.124
  107.7 1.0 select_reduce_fusion.2
  108.7 0.8 fusion.23
  109.5 0.1 copy.67
  109.6 0.1 copy.68
  109.6 0.2 copy.65
  109.8 0.1 reshape.214.w_ref
  110.0 0.8 broadcast_in_dim.128
  110.8 1.1 broadcast_in_dim.129.wl
  111.9 0.0 copy-done.3
  111.9 0.0 copy-start.6
  111.9 17.1 %spread.1 = (f32[256,32,128]{2,1,0:T(8,128)}, f32[16,768,128]{2,1,0:T(8,128)}) custom-call(s32[512]{0:T(512)S(1)} %reshape.208.n_ref, f32[512]{0:T(512)S(1)} %reshape.214.w_ref, bf16[16,1024,128]{2,1,0:T(8,128)(2,1)} %get-tuple-element.18.picked, s32[16,1,1024]{2,1,0:T(1,128)S(1)} %copy-done.3, f32[16,1,1024]{2,1,0:T(1,128)S(1)} %broadcast_in_dim.129.wl, ...), custom_call_target="tpu_custom_call" | custom-call | tf_op jit(solution)/shard_map/spread/pallas_call | solution.py:539
  129.1 0.0 copy-done.6
  129.1 2.2 copy-done.1
  131.2 61.6 %reduce.1 = (f32[512,128]{1,0:T(8,128)S(1)}, bf16[4,384,128]{2,1,0:T(8,128)(2,1)S(1)}) custom-call(f32[16,512,128]{2,1,0:T(8,128)S(1)} %bitcast.59, f32[4,2,1536,128]{3,2,1,0:T(8,128)} %bitcast.65, f32[384,128]{1,0:T(8,128)S(1)} %copy-done.6), custom_call_target="tpu_custom_call" | custom-call | tf_op jit(solution)/shard_map/reduce/pallas_call | solution.py:556
  192.8 3.2 %fusion.3 = f32[16,32,128]{2,1,0:T(8,128)} fusion(f32[16,32,128]{2,1,0:T(8,128)S(1)} %bitcast.63, bf16[16,32,128]{2,1,0:T(8,128)(2,1)S(1)} %copy-done.7, f32[16,32]{1,0:T(8,128)S(1)} %copy-done.11), kind=kOutput, calls=%fused_computation.3 | output fusion | flops 524927 | bytes 657408 | tf_op jit(solution)/shard_map/mul | solution.py:577
  196.1 0.6 convolution_bitcast_fusion.part
  196.6 31.8 %sum.1 = f32[384,128]{1,0:T(8,128)S(1)} custom-call(f32[384,128]{1,0:T(8,128)S(1)} %convolution_bitcast_fusion.part), custom_call_target="tpu_custom_call" | custom-call | tf_op jit(solution)/shard_map/sum/pallas_call | solution.py:585
  228.4 0.7 copy.74
  (22 shorter events, 0.1 us)
Async XLA Ops:
  0.6 1.3 copy-start
  0.6 9.2 %copy-start.9 = (bf16[384,128]{1,0:T(8,128)(2,1)S(1)}, bf16[384,128]{1,0:T(8,128)(2,1)}, u32[]{:S(2)}) copy-start(bf16[384,128]{1,0:T(8,128)(2,1)} %param.8) | copy-start | bytes 294916
  7.2 2.7 %copy-start.10 = (f32[16,32]{1,0:T(8,128)}, f32[16,32]{1,0:T(8,128)S(1)}, u32[]{:S(2)}) copy-start(f32[16,32]{1,0:T(8,128)S(1)} %add_rsqrt_fusion) | copy-start | bytes 6148
  67.3 0.7 copy-start.5
  68.8 4.8 %copy-start.8 = (s32[16,1,32]{0,2,1:T(8,128)}, s32[16,1,32]{0,2,1:T(8,128)S(1)}, u32[]{:S(2)}) copy-start(s32[16,1,32]{0,2,1:T(8,128)S(1)} %copy.58) | copy-start | bytes 6148
  76.5 1.9 copy-start.2
  91.6 0.7 copy-start.4
  92.3 19.7 %copy-start.3 = (s32[16,1,1024]{2,1,0:T(1,128)S(1)}, s32[16,1,1024]{2,1,0:T(1,128)}, u32[]{:S(2)}) copy-start(s32[16,1,1024]{2,1,0:T(1,128)} %reshape.215.idxl) | copy-start | bytes 196612
  111.9 17.1 %copy-start.6 = (f32[384,128]{1,0:T(8,128)S(1)}, f32[384,128]{1,0:T(8,128)}, u32[]{:S(2)}) copy-start(f32[384,128]{1,0:T(8,128)} %copy-done.5) | copy-start | bytes 589828
  129.1 2.2 copy-start.1
  131.2 61.6 %copy-start.7 = (bf16[16,32,128]{2,1,0:T(8,128)(2,1)S(1)}, bf16[16,32,128]{2,1,0:T(8,128)(2,1)}, u32[]{:S(2)}) copy-start(bf16[16,32,128]{2,1,0:T(8,128)(2,1)} %param.9) | copy-start | bytes 393220
  131.2 61.6 %copy-start.11 = (f32[16,32]{1,0:T(8,128)S(1)}, f32[16,32]{1,0:T(8,128)}, u32[]{:S(2)}) copy-start(f32[16,32]{1,0:T(8,128)} %copy-done.10) | copy-start | bytes 6148

commit v2 on v0

v2 whole, which is shorter than its diff:
```python
import functools

import jax
import jax.numpy as jnp
from jax import lax
from jax.experimental import pallas as pl
from jax.experimental.pallas import tpu as pltpu
from jax.sharding import PartitionSpec as P

SOFTMAX_HEAT = 0.5
EPSILON = 1e-06
CAP = 2
X = 4
LANES = 128
SUBS = 4
MESH = pl.DeviceIdType.MESH
VMEM = pl.BlockSpec(memory_space=pltpu.VMEM)
F32, BF16, I32 = jnp.float32, jnp.bfloat16, jnp.int32


def unit_rows(values):
    inverse = lax.rsqrt(jnp.sum(values * values, axis=-1, keepdims=True) + EPSILON)
    return (values * inverse, inverse)


def iota(shape, axis):
    return lax.broadcasted_iota(I32, shape, axis)


def remote(src, dst, send, recv, to):
    return pltpu.make_async_remote_copy(
        src_ref=src, dst_ref=dst, send_sem=send, recv_sem=recv, device_id=to, device_id_type=MESH
    )


def kernel(
    zs, ys,
    states, proj, qraw, idx, nt,
    gq_out, gp_out,
    qall, idxall, ntall, ep, rs, ef, table, kge, kg, wge, wg, picked, qsel, sc, sm, nv, nsm,
    zpart, zseen, ge, gbuf, rbuf, cbuf, sbuf, xbuf, eout, part, abuf, bsrc, bbuf,
    q_s, q_r, e_s, e_r, t_s, t_r, f_s, f_r, i_s, i_r, n_s, n_r, m_s, z_s, z_r,
    g_s, g_r, c_s, c_r, p_s, p_r, y_s, y_r, a_s, a_r, b_s, b_r, o_s, o_r, d_s, d_r,
):
    p = lax.axis_index("pages")
    x, y, z, c = p // (2 * zs), lax.axis_index("queries"), (p // 2) % zs, p % 2

    def at(x_, y_, z_, c_):
        return ((x_ * zs + z_) * 2 + c_, y_)

    def xm(d):
        return (x + d + X) % X

    def ym(d):
        return (y + d + ys) % ys

    def zm(d):
        return (z + d + 2 * zs) % zs

    rows, width = ef.shape
    queries, toks, _ = qraw.shape
    toks_q = queries * toks
    slab = kge.shape[0]
    patches = table.shape[3] * ys // 2
    blocks = ys // 2
    half = zs // 2
    plane = [(dx, dy) for dx in range(X) for dy in range(ys) if dx + dy > 0]
    near_by = [(dx, dc) for dx in range(X) for dc in range(2) if dx + dc > 0]

    barrier = pltpu.get_barrier_semaphore()
    peers = [at(x, y, zm(d), c) for d in range(1, zs)]
    peers += [at(xm(dx), ym(dy), z, c) for dx, dy in plane]
    peers += [at(xm(dx), y, z, 1 - c) for dx in range(X)]
    for to in peers:
        pl.semaphore_signal(barrier, inc=1, device_id=to, device_id_type=MESH)

    qall[z] = unit_rows(qraw[...].astype(F32))[0].astype(BF16)
    ep[...] = jnp.dot(states[...], proj[...], preferred_element_type=F32)
    idxall[z] = idx[z]
    ntall[z] = nt[z]
    sm[...] = jnp.zeros_like(sm)
    pl.semaphore_wait(barrier, len(peers))

    size = queries // SUBS

    def ring(way, s, h, block):
        ref = qall.at[block, pl.ds(h * size, size)]
        k = 0 if way > 0 else 1
        return remote(ref, ref, q_s.at[k, s, h], q_r.at[k, s, h], at(x, y, zm(way), c))

    def ring_parts(way, s):
        if s < half - 1:
            return range(SUBS)
        return range(SUBS // 2) if way > 0 else range(SUBS // 2, SUBS)

    def ring_send(s):
        for h in range(SUBS):
            for way in (1, -1):
                block = zm(-way * s)
                if s > 0:
                    ring(way, s - 1, h, block).wait_recv()
                if h in ring_parts(way, s):
                    ring(way, s, h, block).start()

    ring_send(0)
    e_copies = []
    for d in range(1, ys):
        src = ep.at[pl.ds(pl.multiple_of(ym(d) * rows, 8), rows)]
        to = at(x, ym(d), z, c)
        e_copies.append(remote(src, rs.at[d - 1], e_s.at[d - 1], e_r.at[d - 1], to))
        e_copies[-1].start()
    i_copies = []
    for d in range(1, zs):
        to = at(x, y, zm(d), c)
        for src, dst, s_sem, r_sem in ((idx, idxall, i_s, i_r), (nt, ntall, n_s, n_r)):
            copy = remote(src.at[zm(d)], dst.at[z], s_sem.at[d - 1], r_sem.at[d - 1], to)
            copy.start()
            i_copies.append(copy)
    ring_send(1)
    ring_send(2)

    for copy in e_copies:
        copy.wait_recv()
    own = ep[pl.ds(pl.multiple_of(y * rows, 8), rows), :]
    for d in range(1, ys):
        own = own + rs[d - 1]
    ef[...] = own
    table[x, c, y] = unit_rows(own)[0].astype(BF16)
    mine = table.at[x, c, y]
    t_copies = []
    for i, (dx, dy) in enumerate(plane):
        to = at(xm(dx), ym(dy), z, c)
        t_copies.append(remote(mine, mine, t_s.at[i], t_r.at[i], to))
        t_copies[-1].start()

    def sibling(dx, dy, core):
        i = dx * ys + dy
        ref = table.at[xm(-dx), core, ym(-dy)]
        return remote(ref, ref, f_s.at[i], f_r.at[i], at(x, y, z, 1 - c))

    def forward(dx):
        for dy in range(ys):
            if dx + dy > 0:
                i = plane.index((dx, dy))
                ref = table.at[xm(-dx), c, ym(-dy)]
                remote(ref, ref, t_s.at[i], t_r.at[i], at(x, y, z, 1 - c)).wait_recv()
            sibling(dx, dy, c).start()

    ring_send(3)

    for copy in i_copies:
        copy.wait_recv()
    lane8 = iota((8, LANES), 1)
    for j in range(zs // 2):
        a, b = ((idxall[i] & 1023) - 1 for i in (2 * j, 2 * j + 1))
        kge[0:8, j, :] = jnp.where(lane8 < 64, a, pltpu.roll(b, 64, 1))
        kge[8:16, j, :] = jnp.where(lane8 < 64, pltpu.roll(a, 64, 1), b)
    for s in range(zs):
        nv[s : s + 1, :] = ntall[s]
    lane = iota((zs, LANES), 1)
    number = nv[...]
    valid = (lane < CAP * slab) & (number >= 0)
    teach = pltpu.roll(number, LANES - CAP * slab, 1)
    scalars = pltpu.make_async_copy(idxall, nsm, m_s)
    scalars.start()
    wide = slab * CAP * toks
    lanes = iota((LANES, wide), 1)
    sub = iota((LANES, wide), 0)
    spread = (sub < CAP * slab) & ((sub & (slab - 1)) == (lanes >> 6))
    spread = spread & ((sub >> 4) == ((lanes >> 5) & 1))
    spread = jnp.where(spread, 1.0, 0.0).astype(BF16)
    keys = jnp.dot(
        jnp.where(valid, number, -64.0).astype(BF16), spread, preferred_element_type=F32
    )
    keys = keys.astype(I32) * toks + (iota((zs, wide), 1) & (toks - 1))
    for j in range(wide // LANES):
        kg[:, j, :] = keys[:, j * LANES : (j + 1) * LANES]
    scalars.wait()

    ring_send(4)
    forward(0)
    ring_send(5)
    ring_send(6)
    ring_send(7)
    forward(1)
    for way in (1, -1):
        for h in ring_parts(way, half - 1):
            ring(way, half - 1, h, zm(-way * half)).wait_recv()

    def pick_page(m):
        page = table[m // 4, (m // 2) % 2, pl.ds(blocks * (m % 2), blocks)]
        page = page.reshape(patches, width)
        cols = kge[m].T
        ids = iota((LANES, patches), 1)
        for g in range(zs // 4):
            hot = jnp.concatenate(
                [
                    jnp.where(cols[:, j : j + 1] == ids, 1.0, 0.0).astype(BF16)
                    for j in (2 * g, 2 * g + 1)
                ],
                axis=0,
            )
            got = jnp.dot(hot, page, preferred_element_type=F32)
            picked[m, g * 256 : (g + 1) * 256, :] = got.astype(BF16)
            for i in range(8):
                s = g * 8 + i
                src, k = s // CAP, s % CAP
                query = qall[src, nsm[src, m % 8, m // 8 * (CAP * toks) + k * toks] >> 10]
                qsel[m, s * toks : (s + 1) * toks, :] = query
                sc[k, src : src + 1, :] = jnp.sum(
                    got[i * toks : (i + 1) * toks] * query.astype(F32), axis=0, keepdims=True
                )
        for k in range(CAP):
            col = jnp.sum(sc[k], axis=1, keepdims=True)
            sm[...] = jnp.where(lane == k * slab + m, col, sm[...])

    for dx in range(X):
        if 0 < dx < X - 1:
            forward(dx + 1)
        for dy in range(ys):
            sibling(dx, dy, 1 - c).wait_recv()

        @pl.loop(0, 4)
        def _(i):
            pick_page(xm(-dx) * 4 + i)

    lifted = jnp.where(valid, jnp.exp(sm[...] / SOFTMAX_HEAT), 0.0)
    wide_sum = jnp.zeros((zs, LANES), F32)
    for n in range(16):
        col = jnp.sum(jnp.where(number == n, lifted, 0.0), axis=1, keepdims=True)
        wide_sum = jnp.where((lane & 15) == n, col, wide_sum)
    diagonal = (lane >> 4) == (iota((zs, LANES), 0) & 7)
    wide_sum = jnp.where(diagonal, wide_sum, 0.0)
    for r in range(zs // 8):
        zpart[r : r + 1, :] = jnp.sum(wide_sum[8 * r : 8 * r + 8], axis=0, keepdims=True)
    z_copies = []
    for d in range(1, zs):
        to = at(x, y, zm(d), c)
        z_copies.append(remote(zpart, zseen.at[d - 1], z_s.at[d - 1], z_r.at[d - 1], to))
        z_copies[-1].start()
    total = zpart[...]
    for d in range(1, zs):
        z_copies[d - 1].wait_recv()
        total = total + zseen[d - 1]
    total = jnp.concatenate(
        [jnp.broadcast_to(total[r : r + 1], (8, LANES)) for r in range(zs // 8)], axis=0
    )
    total = jnp.where(diagonal, total, 0.0)
    denom = jnp.ones((zs, LANES), F32)
    for n in range(16):
        col = jnp.sum(jnp.where((lane & 15) == n, total, 0.0), axis=1, keepdims=True)
        denom = jnp.where(valid & (number == n), col, denom)
    weight = jnp.where(valid, (lifted / denom - teach) / SOFTMAX_HEAT, 0.0)
    wide_w = jnp.dot(weight.astype(BF16), spread, preferred_element_type=F32)
    for j in range(wide // LANES):
        wg[:, j, :] = wide_w[:, j * LANES : (j + 1) * LANES]
    turned = weight.T
    wide_w = jnp.zeros((slab, zs * CAP * toks), F32)
    lanes = iota((zs, zs * CAP * toks), 1)
    sub = iota((zs, zs * CAP * toks), 0)
    for k in range(CAP):
        expand = (sub == (lanes >> 6)) & (((lanes >> 5) & 1) == k)
        expand = jnp.where(expand, 1.0, 0.0).astype(BF16)
        wide_w = wide_w + jnp.dot(
            turned[k * slab : (k + 1) * slab].astype(BF16), expand, preferred_element_type=F32
        )
    for j in range(zs * CAP * toks // LANES):
        wge[:, j, :] = wide_w[:, j * LANES : (j + 1) * LANES]

    def hot_pair(key, scale, a, j, ids):
        return jnp.concatenate(
            [
                jnp.where(
                    key[a, pl.ds(i, 1), :] == ids, scale[a, pl.ds(i, 1), :], 0.0
                ).astype(BF16)
                for i in (2 * j, 2 * j + 1)
            ],
            axis=1,
        )

    def query_block(src):
        out = jnp.zeros((toks_q, width), F32)
        ids = iota((toks_q, LANES), 0)
        per = CAP * toks
        first = pl.multiple_of(src * per, per)
        for j in range(wide // 256):
            rows_of = jnp.concatenate(
                [picked[m, pl.ds(first, per), :] for m in range(4 * j, 4 * j + 4)], axis=0
            )
            out = out + jnp.dot(
                hot_pair(kg, wg, src, j, ids), rows_of, preferred_element_type=F32
            )
        gbuf[src] = out

    def page_block(xx, cc, l):
        m = xx * 4 + cc * 2 + l
        out = jnp.zeros((patches, width), F32)
        ids = iota((patches, LANES), 0)
        for j in range(zs * CAP * toks // 256):
            out = out + jnp.dot(
                hot_pair(kge, wge, m, j, ids), qsel[m, j * 256 : (j + 1) * 256, :],
                preferred_element_type=F32,
            )
        ge[xx, cc, l * patches : (l + 1) * patches, :] = out

    part_rows = toks_q // 2

    def gring(way, s, h, begin=False):
        k = 0 if way > 0 else 1
        cut = pl.ds(h * part_rows, part_rows)
        src = gbuf.at[zm(way * (half - s)), cut] if begin else rbuf.at[k, s - 1, cut]
        return remote(
            src, rbuf.at[k, s, cut], g_s.at[k, s, h], g_r.at[k, s, h], at(x, y, zm(way), c)
        )

    def begins(way, h):
        return 0 if (h == 0) == (way > 0) else 1

    def gstep(s):
        if isinstance(s, int) and s == 0:
            query_block(zm(half))
        else:
            query_block(zm(half - s))
            query_block(zm(s - half))
        for h in range(2):
            for way in (1, -1):
                k = 0 if way > 0 else 1
                begin = isinstance(s, int) and s == begins(way, h)
                if isinstance(s, int) and s < begins(way, h):
                    continue
                if not begin:
                    cut = pl.ds(h * part_rows, part_rows)
                    early = isinstance(s, int) and s - 1 == begins(way, h)
                    gring(way, s - 1, h, early).wait_recv()
                    rbuf[k, s - 1, cut] = rbuf[k, s - 1, cut] + gbuf[zm(way * (half - s)), cut]
                gring(way, s, h, begin).start()

    gstep(0)

    def to_sibling(xx):
        return remote(
            ge.at[xx, 1 - c], cbuf.at[xx], c_s.at[xx], c_r.at[xx], at(x, y, z, 1 - c)
        )

    @pl.loop(1, X + 1)
    def _(d):
        for l in range(2):
            page_block(xm(d), 1 - c, l)
        to_sibling(xm(d)).start()

    gstep(1)

    def to_plane(i, xx, yy):
        return remote(sbuf.at[i], xbuf.at[i], p_s.at[i], p_r.at[i], at(xx, yy, z, c))

    @pl.loop(1, X + 1)
    def _(d):
        xx = xm(d)
        for l in range(2):
            page_block(xx, c, l)
        to_sibling(xx).wait_recv()
        for dy in range(ys):
            cut = pl.ds(pl.multiple_of(ym(dy) * rows, 8), rows)
            both = ge[xx, c, cut, :] + cbuf[xx, cut, :]
            i = (d % X) * ys + dy
            sbuf[i] = both.astype(BF16)
            if dy == 0:

                @pl.when(d < X)
                def _():
                    to_plane(i, xx, ym(dy)).start()
            else:
                to_plane(i, xx, ym(dy)).start()

    @pl.loop(2, 5)
    def _(s):
        gstep(s)

    cut = pl.ds(pl.multiple_of(y * rows, 8), rows)
    own = ge[x, c, cut, :] + cbuf[x, cut, :]
    for dx, dy in plane:
        i = dx * ys + dy
        to_plane(i, xm(dx), ym(dy)).wait_recv()
        own = own + xbuf[i].astype(F32)
    unit, inverse = unit_rows(ef[...])
    grad = (own - unit * jnp.sum(unit * own, axis=-1, keepdims=True)) * inverse
    eout[y] = grad.astype(BF16)
    y_copies = []
    for d in range(1, ys):
        to = at(x, ym(d), z, c)
        y_copies.append(remote(eout.at[y], eout.at[y], y_s.at[d - 1], y_r.at[d - 1], to))
        y_copies[-1].start()
    gstep(5)
    for copy in y_copies:
        copy.wait_recv()
    part[...] = lax.dot_general(
        eout[...].reshape(ys * rows, width), states[...], (((0,), (0,)), ((), ())),
        preferred_element_type=F32,
    ).T

    share = part.shape[0] // (2 * X)
    owners = share // 8
    near = [at(xm(dx), y, z, (c + dc) % 2) for dx, dc in near_by]

    def block(k):
        return pl.ds(pl.multiple_of(k * share, 8), share)

    def tile(k):
        return pl.ds(pl.multiple_of(k * 8, 8), 8)

    me = x * 2 + c
    a_copies = []
    for i, (dx, dc) in enumerate(near_by):
        k = xm(dx) * 2 + (c + dc) % 2
        a_copies.append(remote(part.at[block(k)], abuf.at[i], a_s.at[i], a_r.at[i], near[i]))
        a_copies[-1].start()
    gstep(6)
    own = part[block(me), :]
    for i, copy in enumerate(a_copies):
        copy.wait_recv()
        own = own + abuf[i]
    bsrc[...] = own

    def b_copy(k, i, to):
        return remote(bsrc.at[tile(k)], bbuf.at[i], b_s.at[k], b_r.at[i], to)

    for k in range(owners):

        @pl.when(z != k)
        def _():
            b_copy(k, z, at(x, y, k, c)).start()

    gstep(7)
    query_block(z)
    for k, way in ((0, 1), (1, -1)):
        for h in range(2):
            gring(way, half - 1, h).wait_recv()
    unit, inverse = unit_rows(qraw[...].reshape(toks_q, width).astype(F32))

    my_tile = pl.ds(pl.multiple_of(me * share + z * 8, 8), 8)

    def o_copy(i, to):
        return remote(gp_out.at[my_tile], gp_out.at[my_tile], o_s.at[i], o_r.at[z], to)

    @pl.when(z < owners)
    def _():
        total = bsrc[tile(z), :]
        for d in range(1, zs):
            i = zm(d)
            b_copy(0, i, at(x, y, i, c)).wait_recv()
            total = total + bbuf[i]
        gp_out[my_tile, :] = total
        for d in range(1, zs):
            o_copy(d - 1, at(x, y, zm(d), c)).start()

    own = gbuf[z] + rbuf[0, half - 1] + rbuf[1, half - 1]
    gq_out[...] = (own - unit * jnp.sum(unit * own, axis=-1, keepdims=True)) * inverse

    for k in range(owners):

        @pl.when(z != k)
        def _():
            got = gp_out.at[pl.ds(pl.multiple_of(me * share + k * 8, 8), 8)]
            remote(got, got, o_s.at[0], o_r.at[k], at(x, y, k, c)).wait_recv()

    d_copies = []
    for i in range(len(near_by)):
        ref = gp_out.at[block(me)]
        d_copies.append(remote(ref, ref, d_s.at[i], d_r.at[i], near[i]))
        d_copies[-1].start()
    for copy in d_copies:
        copy.wait_recv()

    for s in range(half):
        for way in (1, -1):
            for h in ring_parts(way, s):
                ring(way, s, h, zm(-way * s)).wait_send()
            for h in range(2):
                if s >= begins(way, h):
                    gring(way, s, h, s == begins(way, h)).wait_send()
    for dx in range(X):
        for dy in range(ys):
            sibling(dx, dy, c).wait_send()
            if dx + dy > 0:
                to_plane(dx * ys + dy, xm(dx), ym(dy)).wait_send()
        to_sibling(xm(dx)).wait_send()
    for copy in e_copies + i_copies + t_copies + z_copies + y_copies + a_copies + d_copies:
        copy.wait_send()
    for k in range(owners):

        @pl.when(z != k)
        def _():
            b_copy(k, z, at(x, y, k, c)).wait_send()

    @pl.when(z < owners)
    def _():
        for d in range(1, zs):
            o_copy(d - 1, at(x, y, zm(d), c)).wait_send()


def body(page_states, projection, query_tokens, candidates, patch_index, teacher_logits, page_slot):
    ys = lax.axis_size("queries")
    zs = lax.axis_size("pages") // (2 * X)
    held, patches, share = page_states.shape
    width = projection.shape[1]
    nq, nc, toks = patch_index.shape
    pages = page_slot.shape[0]
    pairs = nq * nc
    chip = 2 * held
    slab = X * chip
    slots = slab * CAP
    rows = held * patches // ys
    half = zs // 2
    per_page = zs * CAP * toks
    near = 2 * X - 1
    block = share // (2 * X)
    S = jax.ShapeDtypeStruct
    V = pltpu.VMEM

    flat = candidates.reshape(pairs)
    ids = jnp.arange(pages, dtype=I32)
    row = jnp.sum(jnp.where(flat[:, None] == ids[None, :], page_slot[None, :], 0), axis=1)
    before = jnp.arange(pairs)[None, :] < jnp.arange(pairs)[:, None]
    arrival = jnp.sum(((row[:, None] == row[None, :]) & before).astype(I32), axis=1)
    owner = (row // chip) % zs
    m = row // (chip * zs) * chip + row % chip
    all_slots = jnp.arange(zs * slots, dtype=I32)[:, None]
    hot = (owner * slots + m % 8 * (2 * CAP) + m // 8 * CAP + arrival)[None, :] == all_slots
    hot2 = (owner * slots + arrival * slab + m)[None, :] == all_slots
    numbers = jnp.arange(pairs, dtype=I32)[None, :] // nc + 1
    number = jnp.sum(jnp.where(hot2, numbers, 0), axis=1) - 1
    probs = jnp.exp(teacher_logits)
    probs = probs / jnp.sum(probs, axis=1, keepdims=True)
    teach = jnp.sum(jnp.where(hot2, probs.reshape(1, pairs), 0.0), axis=1)
    flat_index = patch_index.reshape(pairs, toks) + 1
    asker = jnp.broadcast_to(jnp.arange(pairs, dtype=I32)[:, None] // nc, (pairs, toks))
    digits = jnp.concatenate([flat_index // 32, flat_index % 32, asker], axis=1).astype(BF16)
    digits = jnp.dot(hot.astype(BF16), digits, preferred_element_type=F32)
    digits = digits.astype(I32)
    index = digits[:, :toks] * 32 + digits[:, toks : 2 * toks] + digits[:, 2 * toks :] * 1024
    index = index.reshape(zs, slots * toks // LANES, LANES)
    nt = jnp.concatenate(
        [
            number.astype(F32).reshape(zs, slots),
            teach.reshape(zs, slots),
            jnp.zeros((zs, LANES - 2 * slots), F32),
        ],
        axis=1,
    ).reshape(zs, 1, LANES)

    def dma(*shape):
        return pltpu.SemaphoreType.DMA(shape)

    gq, gp = pl.pallas_call(
        functools.partial(kernel, zs, ys),
        out_shape=(S((nq * toks, width), F32), S((share, width), F32)),
        in_specs=[VMEM] * 5,
        out_specs=(VMEM,) * 2,
        scratch_shapes=[
            V((zs, nq, toks, width), BF16),
            V(index.shape, I32),
            V(nt.shape, F32),
            V((held * patches, width), F32),
            V((ys - 1, rows, width), F32),
            V((rows, width), F32),
            V((X, 2, ys, rows, width), BF16),
            V((slab, zs // 2, LANES), I32),
            V((zs, slots * toks // LANES, LANES), I32),
            V((slab, zs // 2, LANES), F32),
            V((zs, slots * toks // LANES, LANES), F32),
            V((slab, per_page, width), BF16),
            V((slab, per_page, width), BF16),
            V((CAP, zs, LANES), F32),
            V((zs, LANES), F32),
            V((zs, LANES), F32),
            pltpu.SMEM(index.shape, I32),
            V((zs // 8, LANES), F32),
            V((zs - 1, zs // 8, LANES), F32),
            V((X, 2, held * patches, width), F32),
            V((zs, nq * toks, width), F32),
            V((2, half, nq * toks, width), F32),
            V((X, held * patches, width), F32),
            V((X * ys, rows, width), BF16),
            V((X * ys, rows, width), BF16),
            V((ys, rows, width), BF16),
            V((share, width), F32),
            V((near, block, width), F32),
            V((block, width), F32),
            V((zs, 8, width), F32),
            dma(2, half, SUBS), dma(2, half, SUBS),
            dma(ys - 1), dma(ys - 1),
            dma(X * ys - 1), dma(X * ys - 1),
            dma(X * ys), dma(X * ys),
            dma(zs - 1), dma(zs - 1),
            dma(zs - 1), dma(zs - 1),
            pltpu.SemaphoreType.DMA,
            dma(zs - 1), dma(zs - 1),
            dma(2, half, 2), dma(2, half, 2),
            dma(X), dma(X),
            dma(X * ys), dma(X * ys),
            dma(ys - 1), dma(ys - 1),
            dma(near), dma(near),
            dma(block // 8), dma(zs),
            dma(zs), dma(zs),
            dma(near), dma(near),
        ],
        compiler_params=pltpu.CompilerParams(
            collective_id=0, has_side_effects=True, vmem_limit_bytes=56 << 20
        ),
        name="maxsim",
    )(
        page_states.reshape(held * patches, share), projection,
        query_tokens, index, nt,
    )
    return (gq.reshape(nq, toks, width), gp)


def solution(mesh):
    placed = (
        P("pages", None, "queries"),
        P("queries", None),
        P(("pages", "queries"), None, None),
        P(("pages", "queries"), None),
        P(("pages", "queries"), None, None),
        P(("pages", "queries"), None),
        P(),
    )
    return jax.shard_map(
        body,
        mesh=mesh,
        in_specs=placed,
        out_specs=(P(("pages", "queries"), None, None), P("queries", None)),
        check_vma=False,
    )
```

time: 998 us -> 156 us (0.16)
  waiting for transfers between devices: 734 us -> 0 us
  Pallas kernels: 0 us -> 144 us
  local copies, waits for them, and re-layouts: 119 us -> 5.35 us
  starting transfers between devices: 62.9 us -> 0 us
  matrix products: 34 us -> 0.3 us
  between operations: 14.1 us -> 0.71 us
  blocking collectives: 13.2 us -> 0 us
  other arithmetic: 17.3 us -> 4.74 us
    psum x2 -> x0, waiting for transfers between devices: 372 us -> none  [the longest x1 324 us: body(): grad_projection = lax.psum(grad_part, 'pages')]
    all_to_all x4 -> x0, waiting for transfers between devices: 333 us -> none  [the longest x1 172 us: body(): lax.all_to_all(send_query, 'pages', split_axis=1, concat_axis=1, tiled=True)]
    pallas_call x0 -> x1, Pallas kernels: none -> 144 us  [body(): pl.pallas_call(functools.partial(kernel, zs, ys), out_shape=(S((nq * toks...]
    all_to_all x4 -> x0, starting transfers between devices: 62.8 us -> none  [the longest x1 20.4 us: body(): lax.all_to_all(send_index, 'pages', split_axis=1, concat_axis=1, tiled=True)]
    gather x2 -> x0, local copies, waits for them, and re-layouts: 60.6 us -> none  [the longest x1 57.4 us: body(): picked = jnp.take(unit_embed, recv_index + page_base, axis=0)]
    dot_general x12 -> x1, matrix products: 34 us -> 0.3 us  [body(): digits = jnp.dot(hot.astype(BF16), digits, preferred_element_type=F32)]
    scatter x3 -> x0, local copies, waits for them, and re-layouts: 30.2 us -> none  [the longest x1 26.5 us: body(): send_query = jnp.zeros((slot_total, tok_count, embed_width), jnp.bfloat16...]
    all_gather x1 -> x0, waiting for transfers between devices: 28.5 us -> none  [body(): lax.all_gather(flat_states, 'queries', axis=1, tiled=True)]
  transfers between devices with their start and end apart: 7 -> 0, of which waited for: 7 -> 0; matrix products, arithmetic and copies ran while one was open for 6% -> 0% of each run, Pallas kernels for 0% -> 0%
where the time goes in v2:
time: 156 us; the launch traced here: 155 us
  Pallas kernels  144 us (92%)
  local copies, waits for them, and re-layouts  5.35 us (3%)
  other arithmetic  4.74 us (3%)
    pallas_call x1, Pallas kernels, body(): pl.pallas_call(functools.partial(kernel, zs, ys), out_shape=(S((nq * toks...  144 us
    unnamed x2, local copies, waits for them, and re-layouts  3.29 us

profile of v2, /device:TPU:1, one launch (start us, length us, event | category | flops | bytes accessed | tf_op | source)
XLA Modules:
  0.0 155.4 jit_solution(14843819695252975153)
XLA Ops:
  0.6 0.8 exponential_reduce_fusion
  1.4 0.1 pad.2.clone
  1.5 0.8 eq.62
  2.3 0.9 select_reduce_fusion.2
  3.2 0.2 convert_reduce_fusion
  3.4 0.1 select_reduce_fusion.1
  3.6 0.1 convert_element_type.18
  3.6 0.8 exponential_divide_fusion
  4.4 0.1 broadcast_in_dim.63
  4.5 0.2 select_reduce_fusion
  4.7 0.1 reshape.204
  4.7 0.7 maximum_maximum_fusion
  5.4 0.1 broadcast_in_dim.60
  5.5 0.9 broadcast_add_fusion
  6.4 0.1 fusion.2
  6.6 0.3 convolution_convert_fusion
  6.9 0.1 copy.11
  7.0 0.8 reshape.203.idx
  7.8 144.3 %maxsim.1 = (f32[512,128]{1,0:T(8,128)}, f32[384,128]{1,0:T(8,128)}) custom-call(bf16[1536,384]{1,0:T(8,128)(2,1)} %bitcast.29, bf16[384,128]{1,0:T(8,128)(2,1)} %proj.1, bf16[16,32,128]{2,1,0:T(8,128)(2,1)} %qraw.1, s32[16,8,128]{2,1,0:T(8,128)} %reshape.203.idx, f32[16,1,128]{2,1,0:T(1,128)} %bitcast.31), custom_call_target="tpu_custom_call" | custom-call | tf_op jit(solution)/shard_map/maxsim/pallas_call | solution.py:554
  152.1 1.7 %copy.14 = f32[16,32,128]{2,1,0:T(8,128)} copy(f32[16,32,128]{2,1,0:T(8,128)} %bitcast.30) | data formatting | bytes 524288
  153.7 1.6 %copy.15 = f32[384,128]{1,0:T(8,128)} copy(f32[384,128]{1,0:T(8,128)} %get-tuple-element.15) | data formatting | bytes 393216
  (6 shorter events, 0.1 us)

commit v3 on v2

--- a/solution.py
+++ b/solution.py
@@ -31,6 +31,63 @@
     return pltpu.make_async_remote_copy(
         src_ref=src, dst_ref=dst, send_sem=send, recv_sem=recv, device_id=to, device_id_type=MESH
     )
+
+
+def prepare_kernel(zs, slab, toks, cand, pidx, logits, pslot, idx, nt):
+    queries = cand.shape[0]
+    pairs, pages = cand.shape[0] * cand.shape[1], pslot.shape[1]
+    nc = cand.shape[1]
+    chip = slab // X
+    probs = jnp.exp(logits[...])
+    probs = probs / jnp.sum(probs, axis=1, keepdims=True)
+    repeat = jnp.where(iota((nc, pairs), 1) % nc == iota((nc, pairs), 0), 1.0, 0.0)
+    owns = iota((queries, pairs), 1) // nc == iota((queries, pairs), 0)
+
+    def flat(values):
+        wide = jnp.dot(
+            values, repeat, preferred_element_type=F32, precision=lax.Precision.HIGHEST
+        )
+        return jnp.sum(jnp.where(owns, wide, 0.0), axis=0, keepdims=True)
+
+    listed = flat(cand[...].astype(F32)).astype(I32) == iota((pages, pairs), 0)
+    listed = jnp.where(listed, 1.0, 0.0)
+    slot_of = jnp.broadcast_to(pslot[...].astype(F32), (8, pages)).astype(BF16)
+    row = jnp.dot(slot_of, listed.astype(BF16), preferred_element_type=F32)[0:1].astype(I32)
+    before = jnp.where(iota((pairs, pairs), 0) < iota((pairs, pairs), 1), 1.0, 0.0)
+    earlier = jnp.dot(listed.astype(BF16), before.astype(BF16), preferred_element_type=F32)
+    arrival = jnp.sum(earlier * listed, axis=0, keepdims=True).astype(I32)
+    owner = (row // chip) % zs
+    place = row // (chip * zs) * chip + row % chip
+    spot = owner * 8 + (place & 7)
+    turn = (place >> 3) * CAP + arrival
+    patch = pidx[...] + 1
+    asker = iota((pairs, toks), 0) // nc
+    group = iota((pairs, LANES), 1) // toks
+    parts = [
+        jnp.concatenate([v.astype(F32)] * (LANES // toks), axis=1)
+        for v in (patch >> 5, patch & 31, asker)
+    ]
+    sums = [jnp.zeros((zs * 8, LANES), F32) for _ in parts]
+    for u in range(LANES // toks):
+        hot = jnp.where((spot == iota((zs * 8, pairs), 0)) & (turn == u), 1.0, 0.0).astype(BF16)
+        for i, v in enumerate(parts):
+            v = jnp.where(group == u, v, 0.0).astype(BF16)
+            sums[i] = sums[i] + jnp.dot(hot, v, preferred_element_type=F32)
+    high, low, asker = (v.astype(I32) for v in sums)
+    idx[...] = (high * 32 + low + asker * 1024).reshape(idx.shape)
+    turn = arrival * slab + place
+    lines = iota((LANES, pairs), 0)
+    asker = (iota((LANES, pairs), 1) // nc + 1).astype(F32)
+    values = jnp.where(turn == lines, asker, 0.0)
+    values = values + jnp.where(turn + CAP * slab == lines, flat(probs), 0.0)
+    owned = jnp.where(owner == iota((zs, pairs), 0), 1.0, 0.0)
+    tile = lax.dot_general(
+        owned, values, (((1,), (1,)), ((), ())),
+        preferred_element_type=F32, precision=lax.Precision.HIGHEST,
+    )
+    tile = tile - jnp.where(iota((zs, LANES), 1) < CAP * slab, 1.0, 0.0)
+    for s in range(zs):
+        nt[s] = tile[s : s + 1]
 
 
 def kernel(
@@ -76,9 +133,10 @@
 
     qall[z] = unit_rows(qraw[...].astype(F32))[0].astype(BF16)
     ep[...] = jnp.dot(states[...], proj[...], preferred_element_type=F32)
+    sm[...] = jnp.zeros_like(sm)
+
     idxall[z] = idx[z]
     ntall[z] = nt[z]
-    sm[...] = jnp.zeros_like(sm)
     pl.semaphore_wait(barrier, len(peers))
 
     size = queries // SUBS
@@ -92,6 +150,12 @@
         if s < half - 1:
             return range(SUBS)
         return range(SUBS // 2) if way > 0 else range(SUBS // 2, SUBS)
+
+    waiting = []
+
+    def start_some(count):
+        for _ in range(min(count, len(waiting))):
+            waiting.pop(0).start()
 
     def ring_send(s):
         for h in range(SUBS):
@@ -101,14 +165,21 @@
                     ring(way, s - 1, h, block).wait_recv()
                 if h in ring_parts(way, s):
                     ring(way, s, h, block).start()
+            start_some(2)
 
     ring_send(0)
     e_copies = []
-    for d in range(1, ys):
-        src = ep.at[pl.ds(pl.multiple_of(ym(d) * rows, 8), rows)]
-        to = at(x, ym(d), z, c)
-        e_copies.append(remote(src, rs.at[d - 1], e_s.at[d - 1], e_r.at[d - 1], to))
-        e_copies[-1].start()
+    piece = rows // 2
+    for hh in range(2):
+        for d in range(1, ys):
+            src = ep.at[pl.ds(pl.multiple_of(ym(d) * rows + hh * piece, 8), piece)]
+            dst = rs.at[d - 1, pl.ds(hh * piece, piece)]
+            to = at(x, ym(d), z, c)
+            e_copies.append(remote(src, dst, e_s.at[hh, d - 1], e_r.at[hh, d - 1], to))
+            if hh == 0:
+                e_copies[-1].start()
+            else:
+                waiting.append(e_copies[-1])
     i_copies = []
     for d in range(1, zs):
         to = at(x, y, zm(d), c)
@@ -117,21 +188,52 @@
             copy.start()
             i_copies.append(copy)
     ring_send(1)
+
+    t_copies = []
+
+    def pass_on(hh, near, far):
+        dx, dy = (far, near) if hh == 0 else (near, far)
+        i = plane.index((dx, dy))
+        if near == 0:
+            block, to = (x, y), (xm(dx), ym(dy))
+        elif hh == 0:
+            block, to = (xm(-dx), y), (x, ym(dy))
+        else:
+            block, to = (x, ym(-dy)), (xm(dx), y)
+        ref = table.at[block[0], c, block[1], pl.ds(hh * piece, piece)]
+        to = at(*to, z, c)
+        t_copies.append(remote(ref, ref, t_s.at[hh, i], t_r.at[hh, i], to))
+        return t_copies[-1]
+
+    def arrived(hh, dx, dy):
+        i = plane.index((dx, dy))
+        ref = table.at[xm(-dx), c, ym(-dy), pl.ds(hh * piece, piece)]
+        remote(ref, ref, t_s.at[hh, i], t_r.at[hh, i], at(xm(dx), ym(dy), z, c)).wait_recv()
+
+    def relay(hh):
+        for d in range(1, X):
+            arrived(hh, *((d, 0) if hh == 0 else (0, d)))
+            for near in range(1, X):
+                waiting.append(pass_on(hh, near, d))
+
+    def embed(hh):
+        for copy in e_copies[hh * (ys - 1) : (hh + 1) * (ys - 1)]:
+            copy.wait_recv()
+        cut = pl.ds(hh * piece, piece)
+        own = ep[pl.ds(pl.multiple_of(y * rows + hh * piece, 8), piece), :]
+        for d in range(1, ys):
+            own = own + rs[d - 1, cut, :]
+        ef[cut, :] = own
+        table[x, c, y, cut, :] = unit_rows(own)[0].astype(BF16)
+        for d in range(1, X):
+            pass_on(hh, 0, d).start()
+        for d in range(1, X):
+            waiting.append(pass_on(hh, d, 0))
+
+    embed(0)
     ring_send(2)
-
-    for copy in e_copies:
-        copy.wait_recv()
-    own = ep[pl.ds(pl.multiple_of(y * rows, 8), rows), :]
-    for d in range(1, ys):
-        own = own + rs[d - 1]
-    ef[...] = own
-    table[x, c, y] = unit_rows(own)[0].astype(BF16)
-    mine = table.at[x, c, y]
-    t_copies = []
-    for i, (dx, dy) in enumerate(plane):
-        to = at(xm(dx), ym(dy), z, c)
-        t_copies.append(remote(mine, mine, t_s.at[i], t_r.at[i], to))
-        t_copies[-1].start()
+    embed(1)
+    relay(0)
 
     def sibling(dx, dy, core):
         i = dx * ys + dy
@@ -141,13 +243,18 @@
     def forward(dx):
         for dy in range(ys):
             if dx + dy > 0:
-                i = plane.index((dx, dy))
-                ref = table.at[xm(-dx), c, ym(-dy)]
-                remote(ref, ref, t_s.at[i], t_r.at[i], at(x, y, z, 1 - c)).wait_recv()
+                for hh in range(2):
+                    if (dy, dx)[hh] > 0:
+                        arrived(hh, dx, dy)
             sibling(dx, dy, c).start()
 
     ring_send(3)
-
+    relay(1)
+
+    ring_send(4)
+    ring_send(5)
+    forward(0)
+    ring_send(6)
     for copy in i_copies:
         copy.wait_recv()
     lane8 = iota((8, LANES), 1)
@@ -177,11 +284,8 @@
         kg[:, j, :] = keys[:, j * LANES : (j + 1) * LANES]
     scalars.wait()
 
-    ring_send(4)
-    forward(0)
-    ring_send(5)
-    ring_send(6)
     ring_send(7)
+    start_some(len(waiting))
     forward(1)
     for way in (1, -1):
         for h in ring_parts(way, half - 1):
@@ -191,11 +295,12 @@
         page = table[m // 4, (m // 2) % 2, pl.ds(blocks * (m % 2), blocks)]
         page = page.reshape(patches, width)
         cols = kge[m].T
-        ids = iota((LANES, patches), 1)
+        ids = iota((LANES, patches), 1).astype(jnp.int16)
+        one, none = jnp.ones((), BF16), jnp.zeros((), BF16)
         for g in range(zs // 4):
             hot = jnp.concatenate(
                 [
-                    jnp.where(cols[:, j : j + 1] == ids, 1.0, 0.0).astype(BF16)
+                    jnp.where(cols[:, j : j + 1].astype(jnp.int16) == ids, one, none)
                     for j in (2 * g, 2 * g + 1)
                 ],
                 axis=0,
@@ -342,28 +447,16 @@
             ge.at[xx, 1 - c], cbuf.at[xx], c_s.at[xx], c_r.at[xx], at(x, y, z, 1 - c)
         )
 
-    @pl.loop(1, X + 1)
-    def _(d):
-        for l in range(2):
-            page_block(xm(d), 1 - c, l)
-        to_sibling(xm(d)).start()
-
-    gstep(1)
-
     def to_plane(i, xx, yy):
         return remote(sbuf.at[i], xbuf.at[i], p_s.at[i], p_r.at[i], at(xx, yy, z, c))
 
-    @pl.loop(1, X + 1)
-    def _(d):
+    def deliver(d):
         xx = xm(d)
-        for l in range(2):
-            page_block(xx, c, l)
         to_sibling(xx).wait_recv()
         for dy in range(ys):
             cut = pl.ds(pl.multiple_of(ym(dy) * rows, 8), rows)
-            both = ge[xx, c, cut, :] + cbuf[xx, cut, :]
             i = (d % X) * ys + dy
-            sbuf[i] = both.astype(BF16)
+            sbuf[i] = (ge[xx, c, cut, :] + cbuf[xx, cut, :]).astype(BF16)
             if dy == 0:
 
                 @pl.when(d < X)
@@ -372,7 +465,23 @@
             else:
                 to_plane(i, xx, ym(dy)).start()
 
-    @pl.loop(2, 5)
+    @pl.loop(1, X + 2)
+    def _(d):
+        @pl.when(d <= X)
+        def _():
+            for l in range(2):
+                page_block(xm(d), 1 - c, l)
+            to_sibling(xm(d)).start()
+            for l in range(2):
+                page_block(xm(d), c, l)
+
+        @pl.when(d > 1)
+        def _():
+            deliver(d - 1)
+
+    gstep(1)
+
+    @pl.loop(2, 4)
     def _(s):
         gstep(s)
 
@@ -390,7 +499,7 @@
         to = at(x, ym(d), z, c)
         y_copies.append(remote(eout.at[y], eout.at[y], y_s.at[d - 1], y_r.at[d - 1], to))
         y_copies[-1].start()
-    gstep(5)
+    gstep(4)
     for copy in y_copies:
         copy.wait_recv()
     part[...] = lax.dot_general(
@@ -414,7 +523,7 @@
         k = xm(dx) * 2 + (c + dc) % 2
         a_copies.append(remote(part.at[block(k)], abuf.at[i], a_s.at[i], a_r.at[i], near[i]))
         a_copies[-1].start()
-    gstep(6)
+    gstep(5)
     own = part[block(me), :]
     for i, copy in enumerate(a_copies):
         copy.wait_recv()
@@ -430,12 +539,7 @@
         def _():
             b_copy(k, z, at(x, y, k, c)).start()
 
-    gstep(7)
-    query_block(z)
-    for k, way in ((0, 1), (1, -1)):
-        for h in range(2):
-            gring(way, half - 1, h).wait_recv()
-    unit, inverse = unit_rows(qraw[...].reshape(toks_q, width).astype(F32))
+    gstep(6)
 
     my_tile = pl.ds(pl.multiple_of(me * share + z * 8, 8), 8)
 
@@ -453,8 +557,8 @@
         for d in range(1, zs):
             o_copy(d - 1, at(x, y, zm(d), c)).start()
 
-    own = gbuf[z] + rbuf[0, half - 1] + rbuf[1, half - 1]
-    gq_out[...] = (own - unit * jnp.sum(unit * own, axis=-1, keepdims=True)) * inverse
+    gstep(7)
+    query_block(z)
 
     for k in range(owners):
 
@@ -468,6 +572,12 @@
         ref = gp_out.at[block(me)]
         d_copies.append(remote(ref, ref, d_s.at[i], d_r.at[i], near[i]))
         d_copies[-1].start()
+    for way in (1, -1):
+        for h in range(2):
+            gring(way, half - 1, h).wait_recv()
+    unit, inverse = unit_rows(qraw[...].reshape(toks_q, width).astype(F32))
+    own = gbuf[z] + rbuf[0, half - 1] + rbuf[1, half - 1]
+    gq_out[...] = (own - unit * jnp.sum(unit * own, axis=-1, keepdims=True)) * inverse
     for copy in d_copies:
         copy.wait_recv()
 
@@ -504,8 +614,6 @@
     held, patches, share = page_states.shape
     width = projection.shape[1]
     nq, nc, toks = patch_index.shape
-    pages = page_slot.shape[0]
-    pairs = nq * nc
     chip = 2 * held
     slab = X * chip
     slots = slab * CAP
@@ -517,40 +625,18 @@
     S = jax.ShapeDtypeStruct
     V = pltpu.VMEM
 
-    flat = candidates.reshape(pairs)
-    ids = jnp.arange(pages, dtype=I32)
-    row = jnp.sum(jnp.where(flat[:, None] == ids[None, :], page_slot[None, :], 0), axis=1)
-    before = jnp.arange(pairs)[None, :] < jnp.arange(pairs)[:, None]
-    arrival = jnp.sum(((row[:, None] == row[None, :]) & before).astype(I32), axis=1)
-    owner = (row // chip) % zs
-    m = row // (chip * zs) * chip + row % chip
-    all_slots = jnp.arange(zs * slots, dtype=I32)[:, None]
-    hot = (owner * slots + m % 8 * (2 * CAP) + m // 8 * CAP + arrival)[None, :] == all_slots
-    hot2 = (owner * slots + arrival * slab + m)[None, :] == all_slots
-    numbers = jnp.arange(pairs, dtype=I32)[None, :] // nc + 1
-    number = jnp.sum(jnp.where(hot2, numbers, 0), axis=1) - 1
-    probs = jnp.exp(teacher_logits)
-    probs = probs / jnp.sum(probs, axis=1, keepdims=True)
-    teach = jnp.sum(jnp.where(hot2, probs.reshape(1, pairs), 0.0), axis=1)
-    flat_index = patch_index.reshape(pairs, toks) + 1
-    asker = jnp.broadcast_to(jnp.arange(pairs, dtype=I32)[:, None] // nc, (pairs, toks))
-    digits = jnp.concatenate([flat_index // 32, flat_index % 32, asker], axis=1).astype(BF16)
-    digits = jnp.dot(hot.astype(BF16), digits, preferred_element_type=F32)
-    digits = digits.astype(I32)
-    index = digits[:, :toks] * 32 + digits[:, toks : 2 * toks] + digits[:, 2 * toks :] * 1024
-    index = index.reshape(zs, slots * toks // LANES, LANES)
-    nt = jnp.concatenate(
-        [
-            number.astype(F32).reshape(zs, slots),
-            teach.reshape(zs, slots),
-            jnp.zeros((zs, LANES - 2 * slots), F32),
-        ],
-        axis=1,
-    ).reshape(zs, 1, LANES)
-
     def dma(*shape):
         return pltpu.SemaphoreType.DMA(shape)
 
+    index, nt = pl.pallas_call(
+        functools.partial(prepare_kernel, zs, slab, toks),
+        out_shape=(S((zs, 8, LANES), I32), S((zs, 1, LANES), F32)),
+        in_specs=[VMEM] * 4,
+        out_specs=(VMEM,) * 2,
+        name="prepare",
+    )(
+        candidates, patch_index.reshape(nq * nc, toks), teacher_logits, page_slot.reshape(1, -1)
+    )
     gq, gp = pl.pallas_call(
         functools.partial(kernel, zs, ys),
         out_shape=(S((nq * toks, width), F32), S((share, width), F32)),
@@ -558,8 +644,8 @@
         out_specs=(VMEM,) * 2,
         scratch_shapes=[
             V((zs, nq, toks, width), BF16),
-            V(index.shape, I32),
-            V(nt.shape, F32),
+            V((zs, 8, LANES), I32),
+            V((zs, 1, LANES), F32),
             V((held * patches, width), F32),
             V((ys - 1, rows, width), F32),
             V((rows, width), F32),
@@ -573,7 +659,7 @@
             V((CAP, zs, LANES), F32),
             V((zs, LANES), F32),
             V((zs, LANES), F32),
-            pltpu.SMEM(index.shape, I32),
+            pltpu.SMEM((zs, 8, LANES), I32),
             V((zs // 8, LANES), F32),
             V((zs - 1, zs // 8, LANES), F32),
             V((X, 2, held * patches, width), F32),
@@ -588,8 +674,8 @@
             V((block, width), F32),
             V((zs, 8, width), F32),
             dma(2, half, SUBS), dma(2, half, SUBS),
-            dma(ys - 1), dma(ys - 1),
-            dma(X * ys - 1), dma(X * ys - 1),
+            dma(2, ys - 1), dma(2, ys - 1),
+            dma(2, X * ys - 1), dma(2, X * ys - 1),
             dma(X * ys), dma(X * ys),
             dma(zs - 1), dma(zs - 1),
             dma(zs - 1), dma(zs - 1),

time: 156 us -> 142 us (0.910)
  Pallas kernels: 144 us -> 138 us
  other arithmetic: 4.74 us -> 0 us
  local copies, waits for them, and re-layouts: 5.35 us -> 3.29 us
    pallas_call x1, Pallas kernels: 144 us -> 136 us  [body(): pl.pallas_call(functools.partial(kernel, zs, ys), out_shape=(S((nq * toks...]
    pallas_call x0 -> x1, Pallas kernels: none -> 2.72 us  [body(): pl.pallas_call(functools.partial(prepare_kernel, zs, slab, toks), out_sha...]
    reduce_sum x5 -> x0, other arithmetic: 2.17 us -> none  [the longest x1 0.86 us: body(): jnp.sum(jnp.where(flat[:, None] == ids[None, :], page_slot[None, :], 0),...]
where the time goes in v3:
time: 142 us
  Pallas kernels  138 us (97%)
  local copies, waits for them, and re-layouts  3.29 us (2%)
    pallas_call x1, Pallas kernels, body(): pl.pallas_call(functools.partial(kernel, zs, ys), out_shape=(S((nq * toks...  136 us
    unnamed x2, local copies, waits for them, and re-layouts  3.29 us

profile of v3, /device:TPU:1, one launch (start us, length us, event | category | flops | bytes accessed | tf_op | source)
XLA Modules:
  0.0 142.2 jit_solution(12331392669322009607)
XLA Ops:
  0.6 2.7 %prepare.1 = (s32[16,8,128]{2,1,0:T(8,128)}, f32[16,1,128]{2,1,0:T(1,128)}) custom-call(s32[16,16]{1,0:T(8,128)} %cand.1, s32[256,32]{1,0:T(8,128)} %bitcast.6, f32[16,16]{1,0:T(8,128)} %logits.1, s32[1,256]{1,0:T(1,128)} %bitcast.7), custom_call_target="tpu_custom_call" | custom-call | tf_op jit(solution)/shard_map/prepare/pallas_call | solution.py:631
  3.3 135.6 %maxsim.1 = (f32[512,128]{1,0:T(8,128)}, f32[384,128]{1,0:T(8,128)}) custom-call(bf16[1536,384]{1,0:T(8,128)(2,1)} %bitcast.4, bf16[384,128]{1,0:T(8,128)(2,1)} %proj.1, bf16[16,32,128]{2,1,0:T(8,128)(2,1)} %qraw.1, s32[16,8,128]{2,1,0:T(8,128)} %get-tuple-element.6.idx, f32[16,1,128]{2,1,0:T(1,128)} %get-tuple-element.7.nt), custom_call_target="tpu_custom_call" | custom-call | tf_op jit(solution)/shard_map/maxsim/pallas_call | solution.py:640
  139.0 1.7 %copy.11 = f32[16,32,128]{2,1,0:T(8,128)} copy(f32[16,32,128]{2,1,0:T(8,128)} %bitcast.5) | data formatting | bytes 524288
  140.6 1.6 %copy.12 = f32[384,128]{1,0:T(8,128)} copy(f32[384,128]{1,0:T(8,128)} %get-tuple-element.13) | data formatting | bytes 393216

commit v4 on v3

--- a/solution.py
+++ b/solution.py
@@ -606,6 +606,11 @@
     def _():
         for d in range(1, zs):
             o_copy(d - 1, at(x, y, zm(d), c)).wait_send()
+
+
+def store_kernel(a, b, a_out, b_out):
+    a_out[...] = a[...]
+    b_out[...] = b[...]
 
 
 def body(page_states, projection, query_tokens, candidates, patch_index, teacher_logits, page_slot):
@@ -698,6 +703,13 @@
         page_states.reshape(held * patches, share), projection,
         query_tokens, index, nt,
     )
+    gq, gp = pl.pallas_call(
+        store_kernel,
+        out_shape=(S(gq.shape, F32), S(gp.shape, F32)),
+        in_specs=[VMEM] * 2,
+        out_specs=(VMEM,) * 2,
+        name="store",
+    )(gq, gp)
     return (gq.reshape(nq, toks, width), gp)
 
 

time: 142 us -> 141 us (level)
  local copies, waits for them, and re-layouts: 3.29 us -> 0 us
  Pallas kernels: 138 us -> 140 us
    unnamed x2 -> x0, local copies, waits for them, and re-layouts: 3.29 us -> none
    pallas_call x0 -> x1, Pallas kernels: none -> 1.79 us  [body(): pl.pallas_call(store_kernel, out_shape=(S(gq.shape, F32), S(gp.shape, F32...]
where the time goes in v4:
time: 141 us
  Pallas kernels  140 us (99%)
    pallas_call x1, Pallas kernels, body(): pl.pallas_call(functools.partial(kernel, zs, ys), out_shape=(S((nq * toks...  136 us

profile of v4, /device:TPU:1, one launch (start us, length us, event | category | flops | bytes accessed | tf_op | source)
XLA Modules:
  0.0 140.7 jit_solution(3341065634015311945)
XLA Ops:
  0.6 2.7 %prepare.1 = (s32[16,8,128]{2,1,0:T(8,128)}, f32[16,1,128]{2,1,0:T(1,128)}) custom-call(s32[16,16]{1,0:T(8,128)} %cand.1, s32[256,32]{1,0:T(8,128)} %bitcast.5, f32[16,16]{1,0:T(8,128)} %logits.1, s32[1,256]{1,0:T(1,128)} %bitcast.6), custom_call_target="tpu_custom_call" | custom-call | tf_op jit(solution)/shard_map/prepare/pallas_call | solution.py:636
  3.3 135.6 %maxsim.1 = (f32[512,128]{1,0:T(8,128)}, f32[384,128]{1,0:T(8,128)}) custom-call(bf16[1536,384]{1,0:T(8,128)(2,1)} %bitcast.4, bf16[384,128]{1,0:T(8,128)(2,1)} %proj.1, bf16[16,32,128]{2,1,0:T(8,128)(2,1)} %qraw.1, s32[16,8,128]{2,1,0:T(8,128)} %get-tuple-element.8.idx, f32[16,1,128]{2,1,0:T(1,128)} %get-tuple-element.9.nt), custom_call_target="tpu_custom_call" | custom-call | tf_op jit(solution)/shard_map/maxsim/pallas_call | solution.py:645
  139.0 1.8 %store.1 = (f32[512,128]{1,0:T(8,128)}, f32[384,128]{1,0:T(8,128)}) custom-call(f32[512,128]{1,0:T(8,128)} %get-tuple-element.10.a, f32[384,128]{1,0:T(8,128)} %get-tuple-element.11.b), custom_call_target="tpu_custom_call" | custom-call | tf_op jit(solution)/shard_map/store/pallas_call | solution.py:706
